TPU v7x, 256 devices: a whole 4x4x8 slice. The times are simulated.
256 devices in a mesh: dp: 32 (over y, z), uly: 8 (over x, core).
Axes of the slice: x: 4, y: 4, z: 8, core: 2. Of those that a mesh axis runs over, the one named last changes fastest.
Arguments:
- q_video: bfloat16 [32, 1760, 2048], P('dp', 'uly'), may hold values from -6 to 6
- k_video: bfloat16 [32, 1760, 2048], P('dp', 'uly'), may hold values from -6 to 6
- v_video: bfloat16 [32, 1760, 2048], P('dp', 'uly'), may hold values from -6 to 6
- q_audio: bfloat16 [32, 320, 2048], P('dp', 'uly'), may hold values from -6 to 6
- k_audio: bfloat16 [32, 320, 2048], P('dp', 'uly'), may hold values from -6 to 6
- v_audio: bfloat16 [32, 320, 2048], P('dp', 'uly'), may hold values from -6 to 6
- x_video: bfloat16 [32, 1760, 3072], P('dp', 'uly'), may hold values from -3 to 3
- x_audio: bfloat16 [32, 320, 3072], P('dp', 'uly'), may hold values from -3 to 3
- out_video_w: bfloat16 [2048, 3072], P('uly', 'dp'), may hold values from -0.125 to 0.125
- out_audio_w: bfloat16 [2048, 3072], P('uly', 'dp'), may hold values from -0.125 to 0.125
- mod_video: bfloat16 [256, 3072], replicated, may hold values from -0.5 to 0.5
- mod_audio: bfloat16 [256, 3072], replicated, may hold values from -0.5 to 0.5
- slopes: float32 [16], replicated, may hold values from 0.02 to 2
- timesteps: int32 [16], replicated, may hold values from 0 to 999
- pair_ids: int32 [32], P('dp'), may hold values from 0 to 15, as said below
- offsets: int32 [32], P('dp'), may hold values from -160 to 160
Outputs:
- out_video: bfloat16 [32, 1760, 3072], P('dp', 'uly')
- out_audio: bfloat16 [32, 320, 3072], P('dp', 'uly')
Inputs may be any that keep to these rules, and one draw needn't show every extreme that they name: `pair_ids`: each pair number is named by exactly two samples.
All inputs are finite; a program needn't handle non-finite values.
Results may differ from a plain program's by a relative error of at most 0.007.
Values may be sent and summed in bfloat16 or wider, within the bound.
No kernel may reach another device: no remote copies, remote signals or barrier semaphores. Data moves between devices by JAX's collectives and lax.ppermute only.
A program may use at most 192 MiB of HBM per device.

v0:
```python
import math

import jax
import jax.numpy as jnp
from jax import lax
from jax.sharding import PartitionSpec as P

HEADS = 16
HEAD_DIM = 128
FREQ = 256
FRAME_TOK = 880
AUD_FRAME = 160


def inner_rows(left, right):
    return lax.dot_general(
        left, right, (((1,), (1,)), ((), ())), preferred_element_type=jnp.float32
    )


def attend_two(
    query, query_time, keys_v, keys_a, values_v, values_a, time_video, time_audio, slope
):
    scale = 1.0 / math.sqrt(HEAD_DIM)
    scores_v = inner_rows(query, keys_v) * scale - slope * jnp.abs(
        query_time[:, None] - time_video[None, :]
    )
    scores_a = inner_rows(query, keys_a) * scale - slope * jnp.abs(
        query_time[:, None] - time_audio[None, :]
    )
    top = jnp.maximum(
        jnp.max(scores_v, axis=1, keepdims=True), jnp.max(scores_a, axis=1, keepdims=True)
    )
    weights_v = jnp.exp(scores_v - top)
    weights_a = jnp.exp(scores_a - top)
    total = jnp.sum(weights_v, axis=1, keepdims=True) + jnp.sum(weights_a, axis=1, keepdims=True)
    mixed = jnp.dot(weights_v.astype(jnp.bfloat16), values_v, preferred_element_type=jnp.float32)
    mixed = mixed + jnp.dot(
        weights_a.astype(jnp.bfloat16), values_a, preferred_element_type=jnp.float32
    )
    return (mixed / total).astype(jnp.bfloat16)


def attend_blocks(
    query, query_time, keys_v, keys_a, values_v, values_a, time_video, time_audio, slope, block
):
    length = query.shape[0]
    count = length // block
    query_blocks = query.reshape(count, block, query.shape[1])
    time_blocks = query_time.reshape(count, block)

    def one_block(items):
        return attend_two(
            items[0], items[1], keys_v, keys_a, values_v, values_a, time_video, time_audio, slope
        )

    return lax.map(one_block, (query_blocks, time_blocks)).reshape(length, query.shape[1])


def timestep_embed(step_time):
    half = FREQ // 2
    index = jnp.arange(half, dtype=jnp.float32)
    freqs = jnp.exp(-math.log(10000.0) * index / half)
    angles = step_time * freqs
    return jnp.concatenate([jnp.cos(angles), jnp.sin(angles)]).astype(jnp.bfloat16)


def block_product(tokens, weight_blocks, groups):
    rows = tokens.shape[0]
    width = tokens.shape[1] // groups
    left = tokens.reshape(rows, groups, width)
    parts = jnp.einsum(
        "tgw,kgwn->tkgn", left, weight_blocks, preferred_element_type=jnp.float32
    ).astype(jnp.bfloat16)
    summed = jnp.sum(lax.optimization_barrier(parts).astype(jnp.float32), axis=2)
    return summed.reshape(rows, weight_blocks.shape[0] * weight_blocks.shape[3])


def shards(
    q_video,
    k_video,
    v_video,
    q_audio,
    k_audio,
    v_audio,
    x_video,
    x_audio,
    out_video_w,
    out_audio_w,
    mod_video,
    mod_audio,
    slopes,
    timesteps,
    pair_ids,
    offsets,
):
    groups = lax.axis_size("uly")
    position = lax.axis_index("uly")
    own_heads = HEADS // groups
    qv, kv, vv, qa, ka, va = (
        lax.all_to_all(q_video[0], "uly", split_axis=1, concat_axis=0, tiled=True),
        lax.all_to_all(k_video[0], "uly", split_axis=1, concat_axis=0, tiled=True),
        lax.all_to_all(v_video[0], "uly", split_axis=1, concat_axis=0, tiled=True),
        lax.all_to_all(q_audio[0], "uly", split_axis=1, concat_axis=0, tiled=True),
        lax.all_to_all(k_audio[0], "uly", split_axis=1, concat_axis=0, tiled=True),
        lax.all_to_all(v_audio[0], "uly", split_axis=1, concat_axis=0, tiled=True),
    )
    video_len = qv.shape[0]
    audio_len = qa.shape[0]
    video_block = FRAME_TOK
    time_video = (jnp.arange(video_len, dtype=jnp.int32) // FRAME_TOK).astype(jnp.float32)
    time_audio = (jnp.arange(audio_len, dtype=jnp.int32) + offsets[0]).astype(
        jnp.float32
    ) / AUD_FRAME
    own_slopes = lax.dynamic_slice_in_dim(slopes, position * own_heads, own_heads)
    outs_v = []
    outs_a = []
    for head in range(own_heads):
        low = head * HEAD_DIM
        high = low + HEAD_DIM
        keys_v = kv[:, low:high]
        keys_a = ka[:, low:high]
        values_v = vv[:, low:high]
        values_a = va[:, low:high]
        slope = own_slopes[head]
        outs_v.append(
            attend_blocks(
                qv[:, low:high],
                time_video,
                keys_v,
                keys_a,
                values_v,
                values_a,
                time_video,
                time_audio,
                slope,
                video_block,
            )
        )
        outs_a.append(
            attend_blocks(
                qa[:, low:high],
                time_audio,
                keys_v,
                keys_a,
                values_v,
                values_a,
                time_video,
                time_audio,
                slope,
                audio_len,
            )
        )
    attn_video = jnp.concatenate(outs_v, axis=1)
    attn_audio = jnp.concatenate(outs_a, axis=1)
    pair_count = timesteps.shape[0]
    step_time = jnp.sum(
        jnp.where(jnp.arange(pair_count, dtype=jnp.int32) == pair_ids[0], timesteps, 0)
    ).astype(jnp.float32)
    embed = timestep_embed(step_time)[None, :]
    gate_video = jnp.dot(embed, mod_video, preferred_element_type=jnp.float32)
    gate_audio = jnp.dot(embed, mod_audio, preferred_element_type=jnp.float32)
    stacked = jnp.stack((out_video_w, out_audio_w))
    video_rows = x_video.shape[1]
    video_tok, audio_tok = (
        lax.all_to_all(attn_video, "uly", split_axis=0, concat_axis=1, tiled=True),
        lax.all_to_all(attn_audio, "uly", split_axis=0, concat_axis=1, tiled=True),
    )
    group_rows = lax.all_gather(stacked[None], "uly", axis=0, tiled=True)
    piece = lax.all_gather(group_rows[None], "dp", axis=0, tiled=True)
    part_v = block_product(video_tok, piece[:, :, 0], groups)
    part_a = block_product(audio_tok, piece[:, :, 1], groups)
    projected = jnp.concatenate([part_v, part_a], axis=0)
    proj_video = projected[:video_rows]
    proj_audio = projected[video_rows:]
    result_video = (x_video[0].astype(jnp.float32) + gate_video * proj_video).astype(jnp.bfloat16)
    result_audio = (x_audio[0].astype(jnp.float32) + gate_audio * proj_audio).astype(jnp.bfloat16)
    return (result_video[None], result_audio[None])


def solution(mesh):
    return jax.shard_map(
        shards,
        mesh=mesh,
        in_specs=(
            P("dp", "uly", None),
            P("dp", "uly", None),
            P("dp", "uly", None),
            P("dp", "uly", None),
            P("dp", "uly", None),
            P("dp", "uly", None),
            P("dp", "uly", None),
            P("dp", "uly", None),
            P("uly", "dp"),
            P("uly", "dp"),
            P(),
            P(),
            P(),
            P(),
            P("dp"),
            P("dp"),
        ),
        out_specs=(P("dp", "uly", None), P("dp", "uly", None)),
        check_vma=False,
    )
```

profile of v0, /device:TPU:1, one launch (start us, length us, event | category | flops | bytes accessed | tf_op | source)
XLA Modules:
  0.0 277.5 jit_solution(8860125482318583193)
XLA Ops:
  8.2 17.7 %all-gather = bf16[16,256,96]{1,2,0:T(8,128)(2,1)} all-gather(bf16[2,256,96]{1,2,0:T(8,128)(2,1)S(1)} %pad_maximum_fusion.2), channel_id=2, replica_groups=mesh['dp'=32,'uly'=8] {'uly'}, dimensions={0}, use_global_device_ids=true | all-gather | bytes 884736 | tf_op jit(solution)/shard_map/all_gather | solution.py:169
  27.6 3.4 %all-to-all-start.2 = ((bf16[40,8,256]{2,0,1:T(8,128)(2,1)}), bf16[40,8,256]{2,0,1:T(8,128)(2,1)S(1)}, u32[]{:S(2)}, u32[]{:S(2)}) async-start(bf16[40,8,256]{2,0,1:T(8,128)(2,1)} %copy.56), calls=%async_computation.2 | async-start | bytes 327680 | tf_op jit(solution)/shard_map/all_to_all | solution.py:105
  31.8 4.9 %all-to-all-done.2 = bf16[40,8,256]{2,0,1:T(8,128)(2,1)S(1)} async-done(((bf16[40,8,256]{2,0,1:T(8,128)(2,1)}), bf16[40,8,256]{2,0,1:T(8,128)(2,1)S(1)}, u32[]{:S(2)}, u32[]{:S(2)}) %all-to-all-start.2) | async-done | bytes 163872 | tf_op jit(solution)/shard_map/all_to_all | solution.py:105
  37.3 4.2 %all-to-all-start.4 = ((bf16[40,8,256]{2,0,1:T(8,128)(2,1)}), bf16[40,8,256]{2,0,1:T(8,128)(2,1)S(1)}, u32[]{:S(2)}, u32[]{:S(2)}) async-start(bf16[40,8,256]{2,0,1:T(8,128)(2,1)} %copy.58), calls=%async_computation.4 | async-start | bytes 327680 | tf_op jit(solution)/shard_map/all_to_all | solution.py:106
  42.2 4.9 %all-to-all-done.4 = bf16[40,8,256]{2,0,1:T(8,128)(2,1)S(1)} async-done(((bf16[40,8,256]{2,0,1:T(8,128)(2,1)}), bf16[40,8,256]{2,0,1:T(8,128)(2,1)S(1)}, u32[]{:S(2)}, u32[]{:S(2)}) %all-to-all-start.4) | async-done | bytes 163872 | tf_op jit(solution)/shard_map/all_to_all | solution.py:106
  47.1 4.7 %all-to-all-start.6 = ((bf16[40,8,256]{2,0,1:T(8,128)(2,1)}), bf16[40,8,256]{2,0,1:T(8,128)(2,1)}, u32[]{:S(2)}, u32[]{:S(2)}) async-start(bf16[40,8,256]{2,0,1:T(8,128)(2,1)} %copy.60), calls=%async_computation.6 | async-start | bytes 327680 | tf_op jit(solution)/shard_map/all_to_all | solution.py:104
  52.2 1.1 copy.54
  53.3 4.3 %all-to-all-done.6 = bf16[40,8,256]{2,0,1:T(8,128)(2,1)} async-done(((bf16[40,8,256]{2,0,1:T(8,128)(2,1)}), bf16[40,8,256]{2,0,1:T(8,128)(2,1)}, u32[]{:S(2)}, u32[]{:S(2)}) %all-to-all-start.6) | async-done | bytes 163872 | tf_op jit(solution)/shard_map/all_to_all | solution.py:104
  57.6 4.4 %all-to-all-start = ((bf16[220,8,256]{2,0,1:T(8,128)(2,1)}), bf16[220,8,256]{2,0,1:T(8,128)(2,1)S(1)}, u32[]{:S(2)}, u32[]{:S(2)}) async-start(bf16[220,8,256]{2,0,1:T(8,128)(2,1)} %copy.54), calls=%async_computation | async-start | bytes 1835008 | tf_op jit(solution)/shard_map/all_to_all | solution.py:101
  62.3 1.2 copy.57
  66.8 8.8 %all-to-all-done = bf16[220,8,256]{2,0,1:T(8,128)(2,1)S(1)} async-done(((bf16[220,8,256]{2,0,1:T(8,128)(2,1)}), bf16[220,8,256]{2,0,1:T(8,128)(2,1)S(1)}, u32[]{:S(2)}, u32[]{:S(2)}) %all-to-all-start) | async-done | bytes 901152 | tf_op jit(solution)/shard_map/all_to_all | solution.py:101
  75.7 4.3 %all-to-all-start.3 = ((bf16[220,8,256]{2,0,1:T(8,128)(2,1)}), bf16[220,8,256]{2,0,1:T(8,128)(2,1)S(1)}, u32[]{:S(2)}, u32[]{:S(2)}) async-start(bf16[220,8,256]{2,0,1:T(8,128)(2,1)} %copy.57), calls=%async_computation.3 | async-start | bytes 1835008 | tf_op jit(solution)/shard_map/all_to_all | solution.py:103
  80.0 1.4 copy.68
  81.5 1.1 copy.55
  82.6 2.6 copy.52
  85.5 1.9 fusion.138
  87.5 6.2 %all-to-all-done.3 = bf16[220,8,256]{2,0,1:T(8,128)(2,1)S(1)} async-done(((bf16[220,8,256]{2,0,1:T(8,128)(2,1)}), bf16[220,8,256]{2,0,1:T(8,128)(2,1)S(1)}, u32[]{:S(2)}, u32[]{:S(2)}) %all-to-all-start.3) | async-done | bytes 901152 | tf_op jit(solution)/shard_map/all_to_all | solution.py:103
  93.7 4.3 %all-to-all-start.1 = ((bf16[220,8,256]{2,0,1:T(8,128)(2,1)}), bf16[220,8,256]{2,0,1:T(8,128)(2,1)S(1)}, u32[]{:S(2)}, u32[]{:S(2)}) async-start(bf16[220,8,256]{2,0,1:T(8,128)(2,1)} %copy.55), calls=%async_computation.1 | async-start | bytes 1835008 | tf_op jit(solution)/shard_map/all_to_all | solution.py:102
  99.4 2.5 fusion.134
  101.9 2.6 fusion.136
  104.5 1.2 all_to_all.107
  105.8 6.0 %all-to-all-done.1 = bf16[220,8,256]{2,0,1:T(8,128)(2,1)S(1)} async-done(((bf16[220,8,256]{2,0,1:T(8,128)(2,1)}), bf16[220,8,256]{2,0,1:T(8,128)(2,1)S(1)}, u32[]{:S(2)}, u32[]{:S(2)}) %all-to-all-start.1) | async-done | bytes 901152 | tf_op jit(solution)/shard_map/all_to_all | solution.py:102
  111.9 2.1 fusion.129
  114.1 1.3 fusion.127
  116.2 19.3 %while.7 = (s32[]{:T(128)}, bf16[2,880,128]{2,1,0:T(8,128)(2,1)}, bf16[2,880,128]{2,1,0:T(8,128)(2,1)}, bf16[1760,128]{1,0:T(8,128)(2,1)}, f32[]{:T(128)}, /*ind...) while((s32[]{:T(128)}, bf16[2,880,128]{2,1,0:T(8,128)(2,1)}, ...), condition=%wide.region_12.13_spmd.clone, body=%wide.region_7.12_spmd.clone.sunk | while | flops 955821760 | bytes 28645276 | solution.py:57
  116.2 3.3 %fusion.197 = (f32[880]{0:T(1024)S(1)}, f32[880,1760]{1,0:T(8,128)S(1)}) fusion(f32[1760]{0:T(1024)S(1)} %fusion.196, f32[880]{0:T(1024)S(1)} %dynamic-slice_reduce_fusion.5, f32[]{:T(128)} %get-tuple-element.478, bf16[1760,128]{1,0:T(8,128)(2,1)} %get-tuple-element.477, bf16[2,880,128]{2,1,0:T(8,128)(2,1)} %get-tuple-element.476, s32[]{:T(128)S(6)} %copy.85), kind=kOutput, calls=%fused_computation.154.clone.1 | convolution fusion | flops 405784704 | bytes 6885636 | tf_op jit(solution)/shard_map/while/body/eval_jaxpr/dot_general | solution.py:16
  120.2 2.0 fusion.198
  122.2 1.1 fusion.199
  125.9 3.3 %fusion.197 = (f32[880]{0:T(1024)S(1)}, f32[880,1760]{1,0:T(8,128)S(1)}) fusion(f32[1760]{0:T(1024)S(1)} %fusion.196, f32[880]{0:T(1024)S(1)} %dynamic-slice_reduce_fusion.5, f32[]{:T(128)} %get-tuple-element.478, bf16[1760,128]{1,0:T(8,128)(2,1)} %get-tuple-element.477, bf16[2,880,128]{2,1,0:T(8,128)(2,1)} %get-tuple-element.476, s32[]{:T(128)S(6)} %copy.85), kind=kOutput, calls=%fused_computation.154.clone.1 | convolution fusion | flops 405784704 | bytes 6885636 | tf_op jit(solution)/shard_map/while/body/eval_jaxpr/dot_general | solution.py:16
  129.8 2.0 fusion.198
  131.8 1.1 fusion.199
  135.4 1.1 concatenate.25
  137.4 17.6 %while.6 = (s32[]{:T(128)}, bf16[2,880,128]{2,1,0:T(8,128)(2,1)}, bf16[2,880,128]{2,1,0:T(8,128)(2,1)}, bf16[1760,128]{1,0:T(8,128)(2,1)}, f32[]{:T(128)}, /*ind...) while((s32[]{:T(128)}, bf16[2,880,128]{2,1,0:T(8,128)(2,1)}, ...), condition=%wide.region_6.7_spmd.clone, body=%wide.region_1.6_spmd.clone.sunk | while | flops 955821760 | bytes 30448380 | solution.py:57
  137.4 3.4 %fusion.184 = (f32[880]{0:T(1024)S(1)}, f32[880,1760]{1,0:T(8,128)S(1)}) fusion(f32[1760]{0:T(1024)S(1)} %fusion.183, f32[880]{0:T(1024)S(1)} %dynamic-slice_reduce_fusion.4, f32[]{:T(128)} %get-tuple-element.511, bf16[1760,128]{1,0:T(8,128)(2,1)} %get-tuple-element.510, bf16[2,880,128]{2,1,0:T(8,128)(2,1)} %get-tuple-element.509, s32[]{:T(128)S(6)} %copy.91), kind=kOutput, calls=%fused_computation.152.clone.1 | convolution fusion | flops 405784704 | bytes 6885636 | tf_op jit(solution)/shard_map/while/body/eval_jaxpr/dot_general | solution.py:16
  146.2 3.4 %fusion.184 = (f32[880]{0:T(1024)S(1)}, f32[880,1760]{1,0:T(8,128)S(1)}) fusion(f32[1760]{0:T(1024)S(1)} %fusion.183, f32[880]{0:T(1024)S(1)} %dynamic-slice_reduce_fusion.4, f32[]{:T(128)} %get-tuple-element.511, bf16[1760,128]{1,0:T(8,128)(2,1)} %get-tuple-element.510, bf16[2,880,128]{2,1,0:T(8,128)(2,1)} %get-tuple-element.509, s32[]{:T(128)S(6)} %copy.91), kind=kOutput, calls=%fused_computation.152.clone.1 | convolution fusion | flops 405784704 | bytes 6885636 | tf_op jit(solution)/shard_map/while/body/eval_jaxpr/dot_general | solution.py:16
  155.0 1.1 concatenate.24
  157.1 5.0 %all-to-all-start.5 = ((bf16[8,220,256]{2,1,0:T(8,128)(2,1)}), bf16[8,220,256]{2,1,0:T(8,128)(2,1)}, u32[]{:S(2)}, u32[]{:S(2)}) async-start(bf16[8,220,256]{2,1,0:T(8,128)(2,1)} %pad_maximum_fusion), calls=%async_computation.5 | async-start | bytes 1835008 | tf_op jit(solution)/shard_map/all_to_all | solution.py:166
  162.1 2.3 fusion.133
  165.0 2.3 fusion.135
  170.3 39.7 %all-gather.4.cloned.1.call-done = bf16[256,2,256,96]{2,3,1,0:T(8,128)(2,1)} async-done(((bf16[8,2,256,96]{2,3,1,0:T(8,128)(2,1)}), bf16[256,2,256,96]{2,3,1,0:T(8,128)(2,1)}) %all-gather.4.cloned.1.call-update) | async-done | bytes 25165840 | tf_op jit(solution)/shard_map/all_gather | solution.py:170
  210.0 18.3 %fusion.126 = (bf16[32,8,1,256,96]{3,4,2,1,0:T(8,128)(2,1)}, bf16[32,8,1,256,96]{3,4,2,1,0:T(8,128)(2,1)}) fusion(bf16[32,8,2,256,96]{3,4,2,1,0:T(8,128)(2,1)} %bitcast.149), kind=kLoop, calls=%fused_computation.156 | loop fusion | bytes 50331648 | tf_op jit(solution)/shard_map/slice | solution.py:172
  228.3 5.3 %all-to-all-start.7 = ((bf16[8,40,256]{2,1,0:T(8,128)(2,1)}), bf16[8,40,256]{2,1,0:T(8,128)(2,1)S(1)}, u32[]{:S(2)}, u32[]{:S(2)}) async-start(bf16[8,40,256]{2,1,0:T(8,128)(2,1)} %pad_maximum_fusion.1), calls=%async_computation.7 | async-start | bytes 327680 | tf_op jit(solution)/shard_map/all_to_all | solution.py:167
  233.6 9.5 %convert_bitcast_fusion = bf16[220,32,8,96]{0,3,1,2:T(8,128)(2,1)} fusion(bf16[32,8,1,256,96]{3,4,2,1,0:T(8,128)(2,1)} %get-tuple-element.289, bf16[8,220,256]{2,1,0:T(8,128)(2,1)} %all-to-all-done.5), kind=kOutput, calls=%fused_computation.75 | convolution fusion | flops 2773647360 | bytes 24297472 | tf_op jit(solution)/shard_map/tgw,kgwn->tkgn/dot_general | solution.py:72
  243.1 9.4 %convert_reduce_fusion = f32[220,32,96]{0,2,1:T(8,128)} fusion(bf16[220,32,8,96]{0,3,1,2:T(8,128)(2,1)} %convert_bitcast_fusion), kind=kLoop, calls=%fused_computation.70 | loop fusion | flops 10137600 | bytes 13516800 | tf_op jit(solution)/shard_map/reduce_sum | solution.py:75
  252.5 2.4 fusion.59
  254.9 1.5 copy.62
  256.4 10.5 %convert_bitcast_fusion.1 = bf16[40,32,8,96]{3,0,1,2:T(8,128)(2,1)} fusion(bf16[32,8,1,256,96]{3,4,2,1,0:T(8,128)(2,1)} %get-tuple-element.288, bf16[8,40,256]{2,1,0:T(8,128)(2,1)S(1)} %all-to-all-done.7), kind=kOutput, calls=%fused_computation.84 | convolution fusion | flops 504299520 | bytes 14712832 | tf_op jit(solution)/shard_map/tgw,kgwn->tkgn/dot_general | solution.py:72
  266.9 2.5 convert_reduce_fusion.1
  (145 shorter events, 33.3 us)
Async XLA Ops:
  7.2 78.1 %copy-start = (bf16[256,3072]{1,0:T(8,128)(2,1)S(1)}, bf16[256,3072]{1,0:T(8,128)(2,1)}, u32[]{:S(2)}) copy-start(bf16[256,3072]{1,0:T(8,128)(2,1)} %param.30) | copy-start | bytes 4718596
  7.2 23.8 %copy-start.17 = (bf16[1,40,2048]{2,1,0:T(8,128)(2,1)S(1)}, bf16[1,40,2048]{2,1,0:T(8,128)(2,1)}, u32[]{:S(2)}) copy-start(bf16[1,40,2048]{2,1,0:T(8,128)(2,1)} %param.25) | copy-start | bytes 491524
  7.2 34.3 %copy-start.18 = (bf16[1,40,2048]{2,1,0:T(8,128)(2,1)S(1)}, bf16[1,40,2048]{2,1,0:T(8,128)(2,1)}, u32[]{:S(2)}) copy-start(bf16[1,40,2048]{2,1,0:T(8,128)(2,1)} %param.23) | copy-start | bytes 491524
  7.2 202.8 %all-gather.4.cloned.1.call-start = ((), (), s32[]{:S(2)}) async-start(), calls=%async_computation.8 | async-start | bytes 25952256 | tf_op jit(solution)/shard_map/all_gather | solution.py:170
  8.2 43.7 %copy-start.11 = (bf16[1,220,2048]{2,1,0:T(8,128)(2,1)S(1)}, bf16[1,220,2048]{2,1,0:T(8,128)(2,1)}, u32[]{:S(2)}) copy-start(bf16[1,220,2048]{2,1,0:T(8,128)(2,1)} %param.20) | copy-start | bytes 2703364
  27.6 9.0 %all-to-all-start.2 = ((bf16[40,8,256]{2,0,1:T(8,128)(2,1)}), bf16[40,8,256]{2,0,1:T(8,128)(2,1)S(1)}, u32[]{:S(2)}, u32[]{:S(2)}) async-start(bf16[40,8,256]{2,0,1:T(8,128)(2,1)} %copy.56), calls=%async_computation.2 | async-start | bytes 327680 | tf_op jit(solution)/shard_map/all_to_all | solution.py:105
  36.6 0.7 copy-start.13
  37.3 9.8 %all-to-all-start.4 = ((bf16[40,8,256]{2,0,1:T(8,128)(2,1)}), bf16[40,8,256]{2,0,1:T(8,128)(2,1)S(1)}, u32[]{:S(2)}, u32[]{:S(2)}) async-start(bf16[40,8,256]{2,0,1:T(8,128)(2,1)} %copy.58), calls=%async_computation.4 | async-start | bytes 327680 | tf_op jit(solution)/shard_map/all_to_all | solution.py:106
  47.1 6.2 %copy-start.9 = (bf16[40,8,256]{2,0,1:T(8,128)(2,1)}, bf16[40,8,256]{2,0,1:T(8,128)(2,1)S(1)}, u32[]{:S(2)}) copy-start(bf16[40,8,256]{2,0,1:T(8,128)(2,1)S(1)} %all-to-all-done.4) | copy-start | bytes 491524
  47.1 10.5 %all-to-all-start.6 = ((bf16[40,8,256]{2,0,1:T(8,128)(2,1)}), bf16[40,8,256]{2,0,1:T(8,128)(2,1)}, u32[]{:S(2)}, u32[]{:S(2)}) async-start(bf16[40,8,256]{2,0,1:T(8,128)(2,1)} %copy.60), calls=%async_computation.6 | async-start | bytes 327680 | tf_op jit(solution)/shard_map/all_to_all | solution.py:104
  52.1 9.8 %copy-start.12 = (bf16[1,220,2048]{2,1,0:T(8,128)(2,1)S(1)}, bf16[1,220,2048]{2,1,0:T(8,128)(2,1)}, u32[]{:S(2)}) copy-start(bf16[1,220,2048]{2,1,0:T(8,128)(2,1)} %param.22) | copy-start | bytes 2703364
  57.6 18.1 %all-to-all-start = ((bf16[220,8,256]{2,0,1:T(8,128)(2,1)}), bf16[220,8,256]{2,0,1:T(8,128)(2,1)S(1)}, u32[]{:S(2)}, u32[]{:S(2)}) async-start(bf16[220,8,256]{2,0,1:T(8,128)(2,1)} %copy.54), calls=%async_computation | async-start | bytes 1835008 | tf_op jit(solution)/shard_map/all_to_all | solution.py:101
  62.0 2.1 copy-start.21
  62.0 4.1 %copy-start.22 = (f32[16]{0:T(128)S(1)}, f32[16]{0:T(128)}, u32[]{:S(2)}) copy-start(f32[16]{0:T(128)} %param.32) | copy-start | bytes 196
  75.7 18.0 %all-to-all-start.3 = ((bf16[220,8,256]{2,0,1:T(8,128)(2,1)}), bf16[220,8,256]{2,0,1:T(8,128)(2,1)S(1)}, u32[]{:S(2)}, u32[]{:S(2)}) async-start(bf16[220,8,256]{2,0,1:T(8,128)(2,1)} %copy.57), calls=%async_computation.3 | async-start | bytes 1835008 | tf_op jit(solution)/shard_map/all_to_all | solution.py:103
  85.5 12.5 %copy-start.14 = (bf16[40,8,256]{2,0,1:T(8,128)(2,1)S(1)}, bf16[40,8,256]{2,0,1:T(8,128)(2,1)}, u32[]{:S(2)}) copy-start(bf16[40,8,256]{2,0,1:T(8,128)(2,1)} %copy-done.13) | copy-start | bytes 491524
  85.5 13.1 %copy-start.10 = (bf16[40,8,256]{2,0,1:T(8,128)(2,1)S(1)}, bf16[40,8,256]{2,0,1:T(8,128)(2,1)}, u32[]{:S(2)}) copy-start(bf16[40,8,256]{2,0,1:T(8,128)(2,1)} %copy-done.9) | copy-start | bytes 491524
  93.7 18.0 %all-to-all-start.1 = ((bf16[220,8,256]{2,0,1:T(8,128)(2,1)}), bf16[220,8,256]{2,0,1:T(8,128)(2,1)S(1)}, u32[]{:S(2)}, u32[]{:S(2)}) async-start(bf16[220,8,256]{2,0,1:T(8,128)(2,1)} %copy.55), calls=%async_computation.1 | async-start | bytes 1835008 | tf_op jit(solution)/shard_map/all_to_all | solution.py:102
  123.3 1.2 copy-start.7
  123.3 1.2 copy-start.20
  125.0 0.8 copy-start.8
  132.9 1.2 copy-start.7
  132.9 1.2 copy-start.20
  134.7 0.8 copy-start.8
  137.4 4.1 %copy-start.15 = (bf16[2,880,128]{2,1,0:T(8,128)(2,1)S(1)}, bf16[2,880,128]{2,1,0:T(8,128)(2,1)}, u32[]{:S(2)}) copy-start(bf16[2,880,128]{2,1,0:T(8,128)(2,1)} %get-tuple-element.509) | copy-start | bytes 1351684 | tf_op jit(solution)/shard_map/while
  143.7 1.2 copy-start.5
  143.7 1.2 copy-start.19
  145.4 0.8 copy-start.6
  146.2 4.1 %copy-start.15 = (bf16[2,880,128]{2,1,0:T(8,128)(2,1)S(1)}, bf16[2,880,128]{2,1,0:T(8,128)(2,1)}, u32[]{:S(2)}) copy-start(bf16[2,880,128]{2,1,0:T(8,128)(2,1)} %get-tuple-element.509) | copy-start | bytes 1351684 | tf_op jit(solution)/shard_map/while
  152.5 1.2 copy-start.5
  152.5 1.2 copy-start.19
  154.2 0.8 copy-start.6
  157.1 71.2 %all-to-all-start.5 = ((bf16[8,220,256]{2,1,0:T(8,128)(2,1)}), bf16[8,220,256]{2,1,0:T(8,128)(2,1)}, u32[]{:S(2)}, u32[]{:S(2)}) async-start(bf16[8,220,256]{2,1,0:T(8,128)(2,1)} %pad_maximum_fusion), calls=%async_computation.5 | async-start | bytes 1835008 | tf_op jit(solution)/shard_map/all_to_all | solution.py:166
  162.1 2.3 copy-start.3
  165.0 2.4 copy-start.4
  228.3 28.1 %all-to-all-start.7 = ((bf16[8,40,256]{2,1,0:T(8,128)(2,1)}), bf16[8,40,256]{2,1,0:T(8,128)(2,1)S(1)}, u32[]{:S(2)}, u32[]{:S(2)}) async-start(bf16[8,40,256]{2,1,0:T(8,128)(2,1)} %pad_maximum_fusion.1), calls=%async_computation.7 | async-start | bytes 327680 | tf_op jit(solution)/shard_map/all_to_all | solution.py:167
  243.1 9.4 %copy-start.2 = (bf16[1,220,3072]{1,2,0:T(8,128)(2,1)S(1)}, bf16[1,220,3072]{1,2,0:T(8,128)(2,1)}, u32[]{:S(2)}) copy-start(bf16[1,220,3072]{1,2,0:T(8,128)(2,1)} %copy.52) | copy-start | bytes 4055044
  266.9 2.9 %copy-start.16 = (bf16[1,40,3072]{2,1,0:T(8,128)(2,1)S(1)}, bf16[1,40,3072]{2,1,0:T(8,128)(2,1)}, u32[]{:S(2)}) copy-start(bf16[1,40,3072]{2,1,0:T(8,128)(2,1)} %param.27) | copy-start | bytes 737284
  266.9 3.7 %copy-start.1 = (bf16[256,3072]{1,0:T(8,128)(2,1)S(1)}, bf16[256,3072]{1,0:T(8,128)(2,1)}, u32[]{:S(2)}) copy-start(bf16[256,3072]{1,0:T(8,128)(2,1)} %param.30) | copy-start | bytes 4718596
Sparse Core Ops, SparseCore 0:
  26.0 183.9 all-gather.3
where the time goes:
time: 279 us; the launch traced here: 277 us
  waiting for transfers between devices  74.8 us (27%)
  matrix products  59.5 us (21%)
  local copies, waits for them, and re-layouts  46.2 us (17%)
  starting transfers between devices  35.7 us (13%)
  other arithmetic  27 us (10%)
  blocking collectives  17.7 us (6%)
  between operations  16.2 us (6%)
    all_gather x1, waiting for transfers between devices, shards(): piece = lax.all_gather(group_rows[None], 'dp', axis=0, tiled=True)  39.7 us
    dot_general x12, matrix products, inner_rows(): lax.dot_general(left, right, (((1,), (1,)), ((), ())), preferred_element_...  29.2 us
    dot_general x2, matrix products, block_product(): jnp.einsum('tgw,kgwn->tkgn', left, weight_blocks, preferred_element_type=...  20 us
    slice x1, local copies, waits for them, and re-layouts, shards(): part_a = block_product(audio_tok, piece[:, :, 1], groups)  18.3 us
    all_gather x1, blocking collectives, shards(): group_rows = lax.all_gather(stacked[None], 'uly', axis=0, tiled=True)  17.7 us
    reduce_sum x2, other arithmetic, block_product(): jnp.sum(lax.optimization_barrier(parts).astype(jnp.float32), axis=2)  11.9 us
    all_to_all x1, waiting for transfers between devices, shards(): lax.all_to_all(q_video[0], 'uly', split_axis=1, concat_axis=0, tiled=True)  8.84 us
    unnamed x40, local copies, waits for them, and re-layouts  7.7 us
  transfers between devices with their start and end apart: 9, of which 7 were waited for; matrix products, arithmetic and copies ran while one was open for 40% of the time, Pallas kernels for 0%

commit v1 on v0

v1 whole, which is shorter than its diff:
```python
import functools
import math

import jax
import jax.numpy as jnp
from jax import lax
from jax.experimental import pallas as pl
from jax.experimental.pallas import tpu as pltpu
from jax.sharding import PartitionSpec as P

HEADS = 16
HEAD_DIM = 128
FREQ = 256
AUD_FRAME = 160
GROUPS = 8
XS, YS, ZS = 4, 4, 8
VID = 220
AUD = 40
VROWS = 224
AROWS = 48
ROWS = VROWS + AROWS
KEYS = GROUPS * ROWS
LOG2E = math.log2(math.e)
SCALE2 = LOG2E / math.sqrt(HEAD_DIM)
OUTSIDE = 1e30
VMEM = 60 * 2**20


def inner(left, right):
    return lax.dot_general(left, right, (((1,), (1,)), ((), ())), preferred_element_type=jnp.float32)


def pack_kernel(*refs):
    ins, outs = refs[:6], refs[6:]
    for head, out in enumerate(outs):
        for group in range(out.shape[0]):
            source = pl.ds((group * 2 + head) * HEAD_DIM, HEAD_DIM)
            for place in range(3):
                video, audio = ins[place], ins[place + 3]
                lanes = pl.ds(place * HEAD_DIM, HEAD_DIM)
                out[group, VROWS - 16 : VROWS, lanes] = jnp.zeros((16, HEAD_DIM), jnp.bfloat16)
                out[group, ROWS - 16 : ROWS, lanes] = jnp.zeros((16, HEAD_DIM), jnp.bfloat16)
                out[group, 0:VID, lanes] = video[0, :, source]
                out[group, VROWS : VROWS + AUD, lanes] = audio[0, :, source]


def pack(arrays):
    steps = 2
    width = arrays[0].shape[2] // steps
    video = pl.BlockSpec((1, VID, width), lambda g: (0, 0, g))
    audio = pl.BlockSpec((1, AUD, width), lambda g: (0, 0, g))
    out = pl.BlockSpec((GROUPS // steps, ROWS, 3 * HEAD_DIM), lambda g: (g, 0, 0))
    shape = jax.ShapeDtypeStruct((GROUPS, ROWS, 3 * HEAD_DIM), jnp.bfloat16)
    return pl.pallas_call(
        pack_kernel,
        grid=(steps,),
        in_specs=[video] * 3 + [audio] * 3,
        out_specs=[out, out],
        out_shape=[shape, shape],
        compiler_params=pltpu.CompilerParams(vmem_limit_bytes=VMEM),
        cost_estimate=pl.CostEstimate(flops=0, bytes_accessed=1_000_000, transcendentals=0),
    )(*arrays)


def weights_of(scores, bias):
    exponents = scores * SCALE2 - bias
    top = jnp.max(exponents, axis=1, keepdims=True)
    return jnp.exp2(exponents - top).astype(jnp.bfloat16)


def attend_kernel(chip, scalars, key_rows, query, keys, values, *refs):
    outs, out_audio, values_ones = refs[:-2], refs[-2], refs[-1]
    step = pl.program_id(0)
    first = lax.rem(chip[0] + step, XS) * 2

    @pl.when(step == 0)
    def _():
        values_ones[:, :HEAD_DIM] = values[...].reshape(KEYS, HEAD_DIM)
        values_ones[:, HEAD_DIM:] = jnp.ones((KEYS, HEAD_DIM), jnp.bfloat16)

    slope = scalars[0] * LOG2E
    offset = scalars[1]
    key_time = key_rows[0:1, :]
    outside = key_rows[1:2, :]
    all_keys = keys[...].reshape(KEYS, HEAD_DIM)

    def mix(part, query_time):
        bias = slope * jnp.abs(query_time - key_time) + outside
        sums = jnp.dot(
            weights_of(inner(part, all_keys), bias),
            values_ones[...],
            preferred_element_type=jnp.float32,
        )
        return (sums[:, :HEAD_DIM] / sums[:, HEAD_DIM:]).astype(jnp.bfloat16)

    video, times = [], []
    for side in range(2):
        block = first + side
        frame = (block // (GROUPS // 2)).astype(jnp.float32)
        video.append(mix(query[side, :VROWS, :], frame))
        index = lax.broadcasted_iota(jnp.int32, (AROWS, 1), 0) + block * AUD
        times.append((index.astype(jnp.float32) + offset) / AUD_FRAME)
    audio = mix(
        jnp.concatenate([query[side, VROWS:, :] for side in range(2)], axis=0),
        jnp.concatenate(times, axis=0),
    )
    for side in range(2):
        out_audio[first // 2, side] = audio[side * AROWS : (side + 1) * AROWS]
    for dx, out in enumerate(outs):

        @pl.when(step == dx)
        def _(out=out):
            for side in range(2):
                out[side] = video[side]


def attend(chip, scalars, key_rows, qkv):
    video = jax.ShapeDtypeStruct((2, VROWS, HEAD_DIM), jnp.bfloat16)
    return pl.pallas_call(
        attend_kernel,
        grid_spec=pltpu.PrefetchScalarGridSpec(
            num_scalar_prefetch=2,
            grid=(XS,),
            in_specs=[
                pl.BlockSpec((2, KEYS), lambda i, c, s: (0, 0)),
                pl.BlockSpec((2, ROWS, HEAD_DIM), lambda i, c, s: (lax.rem(c[0] + i, XS), 0, 0)),
                pl.BlockSpec((GROUPS, ROWS, HEAD_DIM), lambda i, c, s: (0, 0, 1)),
                pl.BlockSpec((GROUPS, ROWS, HEAD_DIM), lambda i, c, s: (0, 0, 2)),
            ],
            out_specs=[pl.BlockSpec((2, VROWS, HEAD_DIM), lambda i, c, s: (0, 0, 0))] * XS
            + [pl.BlockSpec((XS, 2, AROWS, HEAD_DIM), lambda i, c, s: (0, 0, 0, 0))],
            scratch_shapes=[pltpu.VMEM((KEYS, 2 * HEAD_DIM), jnp.bfloat16)],
        ),
        out_shape=[video] * XS
        + [jax.ShapeDtypeStruct((XS, 2, AROWS, HEAD_DIM), jnp.bfloat16)],
        compiler_params=pltpu.CompilerParams(vmem_limit_bytes=VMEM),
        cost_estimate=pl.CostEstimate(flops=0, bytes_accessed=1_000_000, transcendentals=0),
    )(chip, scalars, key_rows, qkv, qkv, qkv)


def audio_kernel(place, own, other, weight, out, left):
    chip, core = place[0], place[1]
    for half, source in enumerate((own, other)):
        side = core if half == 0 else 1 - core
        for dx in range(XS):
            group = lax.rem(chip - dx + XS, XS) * 2 + side
            for head in range(2):
                low = pl.multiple_of(group * 256 + head * HEAD_DIM, HEAD_DIM)
                left[:, pl.ds(low, HEAD_DIM)] = source[dx, head].reshape(
                    GROUPS * AROWS, HEAD_DIM
                )
    columns = out.shape[2]
    blocks = weight.shape[0] // GROUPS
    rows = [
        weight[group * blocks : (group + 1) * blocks, 0].reshape(columns, 256)
        for group in range(GROUPS)
    ]
    total = inner(left[...], jnp.concatenate(rows, axis=1))
    for device in range(GROUPS):
        out[device] = total[device * AROWS : device * AROWS + AUD].astype(jnp.bfloat16)


def project_audio(place, own, other, weights):
    blocks, slots, width, _ = weights.shape
    whole = pl.BlockSpec(own.shape, lambda n, p: (0,) * own.ndim)
    out = (GROUPS, AUD, blocks // GROUPS * width)
    return pl.pallas_call(
        audio_kernel,
        grid_spec=pltpu.PrefetchScalarGridSpec(
            num_scalar_prefetch=1,
            grid=(1,),
            in_specs=[
                whole,
                whole,
                pl.BlockSpec((blocks, 1, width, 256), lambda n, p: (0, slots - 1, 0, 0)),
            ],
            out_specs=pl.BlockSpec(out, lambda n, p: (0, 0, 0)),
            scratch_shapes=[pltpu.VMEM((GROUPS * AROWS, GROUPS * 256), jnp.bfloat16)],
        ),
        out_shape=jax.ShapeDtypeStruct(out, jnp.bfloat16),
        compiler_params=pltpu.CompilerParams(vmem_limit_bytes=VMEM),
        cost_estimate=pl.CostEstimate(flops=0, bytes_accessed=8_000_000, transcendentals=0),
    )(place, own, other, weights)


def project_kernel(core, *refs):
    sources, weight, own, other, left = refs[: 2 * XS], *refs[2 * XS :]

    @pl.when(pl.program_id(0) == 0)
    def _():
        for half in range(2):
            side = core[0] if half == 0 else 1 - core[0]
            for number, source in enumerate(sources):
                head, dx = divmod(number, XS)
                lanes = pl.ds(dx * 256 + head * HEAD_DIM, HEAD_DIM)
                left[half * VROWS : (half + 1) * VROWS, lanes] = source[side]

    columns = own.shape[1]
    rows = [weight[:, dx].reshape(columns, 256) for dx in range(XS)]
    total = inner(left[...], jnp.concatenate(rows, axis=1))
    own[...] = total[:VROWS].astype(jnp.bfloat16)
    other[...] = total[VROWS:].astype(jnp.bfloat16)


def project(core, sources, weights):
    blocks, _, width, _ = weights.shape
    step = ZS
    out = pl.BlockSpec((VROWS, step * width), lambda n, c: (0, n))
    shape = jax.ShapeDtypeStruct((VROWS, blocks * width), jnp.bfloat16)
    return pl.pallas_call(
        project_kernel,
        grid_spec=pltpu.PrefetchScalarGridSpec(
            num_scalar_prefetch=1,
            grid=(blocks // step,),
            in_specs=[pl.BlockSpec((2, VROWS, HEAD_DIM), lambda n, c: (0, 0, 0))] * (2 * XS)
            + [pl.BlockSpec((step, XS, width, 256), lambda n, c: (n, 0, 0, 0))],
            out_specs=[out, out],
            scratch_shapes=[pltpu.VMEM((2 * VROWS, XS * 256), jnp.bfloat16)],
        ),
        out_shape=[shape, shape],
        compiler_params=pltpu.CompilerParams(vmem_limit_bytes=VMEM),
        cost_estimate=pl.CostEstimate(flops=0, bytes_accessed=25_000_000, transcendentals=0),
    )(core, *sources, weights)


def along(array, axis, shift):
    if axis == "x":
        return lax.ppermute(array, "uly", [(i, (i + 2 * shift) % GROUPS) for i in range(GROUPS)])
    pairs = []
    for i in range(YS * ZS):
        row, column = divmod(i, ZS)
        if axis == "y":
            row = (row + shift) % YS
        else:
            column = (column + shift) % ZS
        pairs.append((i, row * ZS + column))
    return lax.ppermute(array, "dp", pairs)


def after(array, *others):
    return lax.optimization_barrier((array, *others))[0]


def video_kernel(own, other, x, gate, out):
    total = own[...].astype(jnp.float32) + other[...].astype(jnp.float32)
    out[0] = (x[0].astype(jnp.float32) + gate[...] * total[:VID]).astype(jnp.bfloat16)


def finish_video(own, other, x, gate):
    total = own.shape[1]
    step = total // 4
    half = pl.BlockSpec((VROWS, step), lambda n: (0, n))
    video = pl.BlockSpec((1, VID, step), lambda n: (0, 0, n))
    return pl.pallas_call(
        video_kernel,
        grid=(4,),
        in_specs=[half, half, video, pl.BlockSpec((1, step), lambda n: (0, n))],
        out_specs=video,
        out_shape=jax.ShapeDtypeStruct(x.shape, jnp.bfloat16),
        compiler_params=pltpu.CompilerParams(vmem_limit_bytes=VMEM // 4),
        cost_estimate=pl.CostEstimate(flops=0, bytes_accessed=6_000_000, transcendentals=0),
    )(own, other, x, gate)


def place_kernel(parts, x, gate, out):
    total = jnp.concatenate([parts[i] for i in range(GROUPS)], axis=1).astype(jnp.float32)
    out[0] = (x[0].astype(jnp.float32) + gate[...] * total).astype(jnp.bfloat16)


def finish_audio(parts, x, gate):
    return pl.pallas_call(
        place_kernel,
        out_shape=jax.ShapeDtypeStruct(x.shape, jnp.bfloat16),
        compiler_params=pltpu.CompilerParams(vmem_limit_bytes=VMEM // 4),
        cost_estimate=pl.CostEstimate(flops=0, bytes_accessed=3_000_000, transcendentals=0),
    )(parts, x, gate)


def timestep_embed(step_time):
    half = FREQ // 2
    index = jnp.arange(half, dtype=jnp.float32)
    freqs = jnp.exp(-math.log(10000.0) * index / half)
    angles = step_time * freqs
    return jnp.concatenate([jnp.cos(angles), jnp.sin(angles)]).astype(jnp.bfloat16)


def key_table(offset):
    index = jnp.arange(KEYS, dtype=jnp.int32)
    block, row = index // ROWS, index % ROWS
    is_video = row < VROWS
    video_time = (block // (GROUPS // 2)).astype(jnp.float32)
    audio_time = (block * AUD + (row - VROWS) + offset).astype(jnp.float32) / AUD_FRAME
    filling = (is_video & (row >= VID)) | (row >= VROWS + AUD)
    return jnp.stack(
        [jnp.where(is_video, video_time, audio_time), jnp.where(filling, OUTSIDE, 0.0)]
    ).astype(jnp.float32)


def shards(
    q_video,
    k_video,
    v_video,
    q_audio,
    k_audio,
    v_audio,
    x_video,
    x_audio,
    out_video_w,
    out_audio_w,
    mod_video,
    mod_audio,
    slopes,
    timesteps,
    pair_ids,
    offsets,
):
    position = lax.axis_index("uly")
    outer = lax.axis_index("dp")
    core = (position % 2).astype(jnp.int32)
    chip = (position // 2).astype(jnp.int32)
    own_heads = HEADS // GROUPS
    swap = [(i, i ^ 1) for i in range(GROUPS)]
    shifts = (1, 2, -1)

    block = out_video_w.T
    slots = [block] + [along(block, "x", shift) for shift in shifts]
    own_blocks = YS * ZS // GROUPS
    moves = []
    for column in range(YS * ZS):
        for group in range(GROUPS):
            over = group // 2 * ZS + group % 2 * own_blocks + column % own_blocks
            moves.append((column * GROUPS + group, over * GROUPS + column // own_blocks))
    slots.append(lax.ppermute(out_audio_w.T, ("dp", "uly"), moves))
    weights = lax.all_gather(jnp.stack(slots), "dp", axis=0, tiled=False)

    packed = pack((q_video, k_video, v_video, q_audio, k_audio, v_audio))
    qkv = [None, None]
    qkv[0] = lax.all_to_all(packed[0], "uly", split_axis=0, concat_axis=0, tiled=True)

    pair_count = timesteps.shape[0]
    step_time = jnp.sum(
        jnp.where(jnp.arange(pair_count, dtype=jnp.int32) == pair_ids[0], timesteps, 0)
    ).astype(jnp.float32)
    embed = timestep_embed(step_time)[None, :]
    gate_v = jnp.dot(embed, mod_video, preferred_element_type=jnp.float32)
    gate_a = jnp.dot(embed, mod_audio, preferred_element_type=jnp.float32)
    key_rows = key_table(offsets[0])
    offset = offsets[0].astype(jnp.float32)

    def attention(head, qkv):
        scalars = jnp.stack([slopes[position * own_heads + head], offset])
        *video, audio = attend(chip[None], scalars, key_rows, qkv)
        sent = [along(array, "x", dx) if dx else array for dx, array in enumerate(video)]
        return sent, audio, video[0]

    first, gate_v, gate_a, key_rows = lax.optimization_barrier((qkv[0], gate_v, gate_a, key_rows))
    qkv[1] = lax.all_to_all(
        after(packed[1], first), "uly", split_axis=0, concat_axis=0, tiled=True
    )
    sent0, audio0, done = attention(0, first)
    sent1, audio1, _ = attention(1, after(qkv[1], done))
    audio = jnp.stack([audio0, audio1])
    audio = jnp.stack([audio] + [along(audio, "x", shift) for shift in shifts])
    other_audio = lax.ppermute(audio, "uly", swap)
    parts = project_audio(jnp.stack([chip, core]), audio, other_audio, weights)
    sources = sent0 + sent1
    sources[0] = after(sources[0], parts)
    parts = lax.all_to_all(parts, "uly", split_axis=0, concat_axis=0, tiled=True)
    own, other = project(core[None], sources, weights)
    received = lax.ppermute(other, "uly", swap)
    out_audio = finish_audio(parts, x_audio, gate_a)
    return finish_video(own, received, x_video, gate_v), out_audio


def solution(mesh):
    tokens = P("dp", "uly", None)
    return jax.shard_map(
        shards,
        mesh=mesh,
        in_specs=(tokens,) * 8 + (P("uly", "dp"), P("uly", "dp")) + (P(),) * 4 + (P("dp"), P("dp")),
        out_specs=(tokens, tokens),
        check_vma=False,
    )
```

time: 279 us -> 161 us (0.58)
  matrix products: 59.5 us -> 0.63 us
  local copies, waits for them, and re-layouts: 46.2 us -> 4.14 us
  Pallas kernels: 0 us -> 40.5 us
  waiting for transfers between devices: 74.8 us -> 41.2 us
  other arithmetic: 27 us -> 4.98 us
  blocking collectives: 17.7 us -> 10.5 us
  starting transfers between devices: 35.7 us -> 42.5 us
    dot_general x28 -> x2, matrix products: 59.5 us -> 0.63 us  [the longest x1 0.32 us: shards(): gate_a = jnp.dot(embed, mod_audio, preferred_element_type=jnp.float32)]
    pallas_call x0 -> x7, Pallas kernels: none -> 40.5 us  [the longest x2 22 us: attend(): pl.pallas_call(attend_kernel, grid_spec=pltpu.PrefetchScalarGridSpec(num_...]
    all_gather x1, waiting for transfers between devices: 39.7 us -> 5.06 us  [shards(): weights = lax.all_gather(jnp.stack(slots), 'dp', axis=0, tiled=False)]
    ppermute x0 -> x15, starting transfers between devices: none -> 30.2 us  [the longest x12 16.8 us: along(): lax.ppermute(array, 'uly', [(i, (i + 2 * shift) % GROUPS) for i in range(...]
    slice x6 -> x0, local copies, waits for them, and re-layouts: 23.7 us -> none  [the longest x1 18.3 us: shards(): part_a = block_product(audio_tok, piece[:, :, 1], groups)]
    all_to_all x8 -> x2, starting transfers between devices: 35.7 us -> 12.3 us  [the longest x1 7.14 us: shards(): lax.all_to_all(packed[0], 'uly', split_axis=0, concat_axis=0, tiled=True)]
    reduce_sum x14 -> x0, other arithmetic: 17.7 us -> none  [the longest x2 11.9 us: block_product(): jnp.sum(lax.optimization_barrier(parts).astype(jnp.float32), axis=2)]
    all_gather x1 -> x0, blocking collectives: 17.7 us -> none  [shards(): group_rows = lax.all_gather(stacked[None], 'uly', axis=0, tiled=True)]
  transfers between devices with their start and end apart: 9 -> 18, of which waited for: 7 -> 7; matrix products, arithmetic and copies ran while one was open for 40% -> 4% of each run, Pallas kernels for 0% -> 19%
where the time goes in v1:
time: 161 us
  starting transfers between devices  42.5 us (26%)
  waiting for transfers between devices  41.2 us (26%)
  Pallas kernels  40.5 us (25%)
  between operations  16.2 us (10%)
  blocking collectives  10.5 us (7%)
  other arithmetic  4.98 us (3%)
  local copies, waits for them, and re-layouts  4.14 us (3%)
    pallas_call x2, Pallas kernels, attend(): pl.pallas_call(attend_kernel, grid_spec=pltpu.PrefetchScalarGridSpec(num_...  22 us
    all_to_all x1, waiting for transfers between devices, shards(): lax.all_to_all(packed[0], 'uly', split_axis=0, concat_axis=0, tiled=True)  17.8 us
    ppermute x12, starting transfers between devices, along(): lax.ppermute(array, 'uly', [(i, (i + 2 * shift) % GROUPS) for i in range(...  16.8 us
    all_to_all x1, blocking collectives, shards(): lax.all_to_all(parts, 'uly', split_axis=0, concat_axis=0, tiled=True)  10.5 us
    ppermute x1, starting transfers between devices, shards(): slots.append(lax.ppermute(out_audio_w.T, ('dp', 'uly'), moves))  10.2 us
    ppermute x12, waiting for transfers between devices, along(): lax.ppermute(array, 'uly', [(i, (i + 2 * shift) % GROUPS) for i in range(...  8.68 us
    all_to_all x1, waiting for transfers between devices, shards(): lax.all_to_all(after(packed[1], first), 'uly', split_axis=0, concat_axis=...  8.51 us
    pallas_call x1, Pallas kernels, project(): pl.pallas_call(project_kernel, grid_spec=pltpu.PrefetchScalarGridSpec(num...  7.36 us
  transfers between devices with their start and end apart: 18, of which 7 were waited for; matrix products, arithmetic and copies ran while one was open for 4% of the time, Pallas kernels for 19%

profile of v1, /device:TPU:1, one launch (start us, length us, event | category | flops | bytes accessed | tf_op | source)
XLA Modules:
  0.0 160.6 jit_solution(14421208366856154889)
XLA Ops:
  7.2 0.0 all-gather.3.cloned.1.call-start
  7.2 2.1 %collective-permute-start.4 = (bf16[96,256]{1,0:T(8,128)(2,1)}, bf16[96,256]{1,0:T(8,128)(2,1)S(1)}, u32[]{:S(2)}, u32[]{:S(2)}) collective-permute-start(bf16[96,256]{1,0:T(8,128)(2,1)} %bitcast.42), channel_id=1, source_target_pairs={{0,2},{1,3},{2,4},{3,5},{4,6},{5,7},{6,0},{7,1},{8,10},{9,11},{10,... | collective-permute-start | bytes 147464 | tf_op jit(solution)/shard_map/ppermute | solution.py:228
  9.3 2.5 %collective-permute-start.5 = (bf16[96,256]{1,0:T(8,128)(2,1)}, bf16[96,256]{1,0:T(8,128)(2,1)S(1)}, u32[]{:S(2)}, u32[]{:S(2)}) collective-permute-start(bf16[96,256]{1,0:T(8,128)(2,1)} %bitcast.43), channel_id=1, source_target_pairs={{0,4},{1,5},{2,6},{3,7},{4,0},{5,1},{6,2},{7,3},{8,12},{9,13},{10,... | collective-permute-start | bytes 147464 | tf_op jit(solution)/shard_map/ppermute | solution.py:228
  11.8 1.2 collective-permute-start.6
  12.9 10.2 %collective-permute-start.7 = (bf16[96,256]{1,0:T(8,128)(2,1)}, bf16[96,256]{1,0:T(8,128)(2,1)S(1)}, u32[]{:S(2)}, u32[]{:S(2)}) collective-permute-start(bf16[96,256]{1,0:T(8,128)(2,1)} %bitcast.45), channel_id=1, source_target_pairs={{0,0},{1,32},{2,64},{3,96},{4,128},{5,160},{6,192},{7,224},{8,8},{... | collective-permute-start | bytes 147464 | tf_op jit(solution)/shard_map/ppermute | solution.py:333
  23.2 0.8 bitcast_dynamic-update-slice_fusion
  24.0 1.1 collective-permute-done.7
  25.1 0.7 copy-done.8
  25.9 3.5 %shard_map.167 = (bf16[8,272,384]{2,1,0:T(8,128)(2,1)}, bf16[8,272,384]{2,1,0:T(8,128)(2,1)}) custom-call(bf16[1,220,2048]{2,1,0:T(8,128)(2,1)} %refs_0_.1, bf16[1,220,2048]{2,1,0:T(8,128)(2,1)} %refs_1_.1, bf16[1,220,2048]{2,1,0:T(8,128)(2,1)} %refs_2_.1, bf16[1,40,2048]{2,1,0:T(8,128)(2,1)} %refs_3_.1, bf16[1,40,2048]{2,1,0:T(8,128)(2,1)} %refs_4_.1, ...), custom_call_target="tpu_custom_call" | custom-call | bytes 1000000 | tf_op jit(solution)/shard_map/pallas_call | solution.py:54
  29.3 7.1 %all-to-all-start = ((bf16[8,272,384]{2,1,0:T(8,128)(2,1)}), bf16[8,272,384]{2,1,0:T(8,128)(2,1)}, u32[]{:S(2)}, u32[]{:S(2)}) async-start(bf16[8,272,384]{2,1,0:T(8,128)(2,1)} %get-tuple-element.23), calls=%async_computation | async-start | bytes 3342336 | tf_op jit(solution)/shard_map/all_to_all | solution.py:338
  37.3 0.6 fusion
  39.1 0.1 sine_convert_fusion
  39.2 0.3 fusion.3.gate
  39.5 0.3 fusion.4.gate
  39.8 0.1 or_select_fusion
  39.9 0.6 pad_maximum_fusion.2.key_rows
  40.6 17.8 %all-to-all-done.query.keys.values = bf16[8,272,384]{2,1,0:T(8,128)(2,1)} async-done(((bf16[8,272,384]{2,1,0:T(8,128)(2,1)}), bf16[8,272,384]{2,1,0:T(8,128)(2,1)}, u32[]{:S(2)}, u32[]{:S(2)}) %all-to-all-start) | async-done | bytes 1671200 | tf_op jit(solution)/shard_map/all_to_all | solution.py:338
  58.4 5.2 %all-to-all-start.1 = ((bf16[8,272,384]{2,1,0:T(8,128)(2,1)}), bf16[8,272,384]{2,1,0:T(8,128)(2,1)}, u32[]{:S(2)}, u32[]{:S(2)}) async-start(bf16[8,272,384]{2,1,0:T(8,128)(2,1)} %get-tuple-element.29), calls=%async_computation.1 | async-start | bytes 3342336 | tf_op jit(solution)/shard_map/all_to_all | solution.py:357
  63.5 0.6 fusion.2
  64.1 1.9 %pad_maximum_fusion.3 = (f32[2]{0:T(128)}, f32[2]{0:T(128)}) fusion(f32[1]{0:T(128)} %get-tuple-element.47, f32[1]{0:T(128)} %bitcast.3, f32[1]{0:T(128)} %get-tuple-element.46), kind=kLoop, calls=%fused_computation.21 | loop fusion | flops 4 | bytes 28 | tf_op jit(solution)/shard_map/stack | solution.py:351
  66.0 10.9 %shard_map.168 = (bf16[2,224,128]{2,1,0:T(8,128)(2,1)}, bf16[2,224,128]{2,1,0:T(8,128)(2,1)}, bf16[2,224,128]{2,1,0:T(8,128)(2,1)}, bf16[2,224,128]{2,1,0:T(8,128)(2,1)}, bf16[4,2,48,128]{3,2,1,0:T(8,128)(2,1)}) custom-call(s32[1]{0:T(128)} %bitcast.1.chip, f32[2]{0:T(128)} %get-tuple-element.48.scalars, f32[2,2176]{1,0:T(2,128)} %pad_maximum_fusion.2.key_rows, ...), custom_call_target="tpu_custom_call" | custom-call | bytes 1000000 | tf_op jit(solution)/shard_map/pallas_call | solution.py:119
  76.9 8.5 %all-to-all-done.1.query.keys.values = bf16[8,272,384]{2,1,0:T(8,128)(2,1)} async-done(((bf16[8,272,384]{2,1,0:T(8,128)(2,1)}), bf16[8,272,384]{2,1,0:T(8,128)(2,1)}, u32[]{:S(2)}, u32[]{:S(2)}) %all-to-all-start.1) | async-done | bytes 1671200 | tf_op jit(solution)/shard_map/all_to_all | solution.py:357
  85.4 11.1 %shard_map.169 = (bf16[2,224,128]{2,1,0:T(8,128)(2,1)}, bf16[2,224,128]{2,1,0:T(8,128)(2,1)}, bf16[2,224,128]{2,1,0:T(8,128)(2,1)}, bf16[2,224,128]{2,1,0:T(8,128)(2,1)}, bf16[4,2,48,128]{3,2,1,0:T(8,128)(2,1)}) custom-call(s32[1]{0:T(128)} %bitcast.1.chip, f32[2]{0:T(128)} %get-tuple-element.49.scalars, f32[2,2176]{1,0:T(2,128)} %pad_maximum_fusion.2.key_rows, ...), custom_call_target="tpu_custom_call" | custom-call | bytes 1000000 | tf_op jit(solution)/shard_map/pallas_call | solution.py:119
  96.5 1.0 fusion.1
  97.5 0.4 collective-permute-start
  97.9 1.8 %collective-permute-start.1 = (bf16[2,4,2,48,128]{4,3,2,1,0:T(8,128)(2,1)S(1)}, bf16[2,4,2,48,128]{4,3,2,1,0:T(8,128)(2,1)S(1)}, u32[]{:S(2)}, u32[]{:S(2)}) collective-permute-start(bf16[2,4,2,48,128]{4,3,2,1,0:T(8,128)(2,1)S(1)} %get-tuple-element.45), channel_id=1, source_target_pairs={{0,4},{1,5},{2,6},{3,7},{4,0},{5,1},{6,2},{7,3},{8,12},{9,13},{10,... | collective-permute-start | bytes 589832 | tf_op jit(solution)/shard_map/ppermute | solution.py:228
  99.6 0.7 collective-permute-start.2
  100.4 4.7 %collective-permute-done = bf16[2,4,2,48,128]{4,3,2,1,0:T(8,128)(2,1)S(1)} collective-permute-done((bf16[2,4,2,48,128]{4,3,2,1,0:T(8,128)(2,1)S(1)}, bf16[2,4,2,48,128]{4,3,2,1,0:T(8,128)(2,1)S(1)}, u32[]{:S(2)}, u32[]{:S(2)}) %collective-permute-start) | collective-permute-done | bytes 196640 | tf_op jit(solution)/shard_map/ppermute | solution.py:228
  105.1 2.9 %collective-permute-done.1 = bf16[2,4,2,48,128]{4,3,2,1,0:T(8,128)(2,1)S(1)} collective-permute-done((bf16[2,4,2,48,128]{4,3,2,1,0:T(8,128)(2,1)S(1)}, bf16[2,4,2,48,128]{4,3,2,1,0:T(8,128)(2,1)S(1)}, u32[]{:S(2)}, u32[]{:S(2)}) %collective-permute-start.1) | collective-permute-done | bytes 196640 | tf_op jit(solution)/shard_map/ppermute | solution.py:228
  108.0 1.0 collective-permute-done.2
  109.0 0.1 pad_maximum_fusion.own
  109.1 2.0 %collective-permute-start.3 = (bf16[4,2,4,2,48,128]{5,4,3,2,1,0:T(8,128)(2,1)S(1)}, bf16[4,2,4,2,48,128]{5,4,3,2,1,0:T(8,128)(2,1)S(1)}, u32[]{:S(2)}, u32[]{:S(2)}) collective-permute-start(bf16[4,2,4,2,48,128]{5,4,3,2,1,0:T(8,128)(2,1)S(1)} %pad_maximum_fusion.own), channel_id=1, source_target_pairs={{0,1},{1,0},{2,3},{3,2},{4,5},{5,4},{6,7},{7,6},{8,9},{9,8},{10,11... | collective-permute-start | bytes 2359304 | tf_op jit(solution)/shard_map/ppermute | solution.py:364
  111.2 2.2 %collective-permute-start.10 = (bf16[2,224,128]{2,1,0:T(8,128)(2,1)S(1)}, bf16[2,224,128]{2,1,0:T(8,128)(2,1)S(1)}, u32[]{:S(2)}, u32[]{:S(2)}) collective-permute-start(bf16[2,224,128]{2,1,0:T(8,128)(2,1)S(1)} %copy-done.14), channel_id=1, source_target_pairs={{0,6},{1,7},{2,0},{3,1},{4,2},{5,3},{6,4},{7,5},{8,14},{9,15},{10,... | collective-permute-start | bytes 344072 | tf_op jit(solution)/shard_map/ppermute | solution.py:228
  113.3 1.2 collective-permute-start.9
  114.5 2.1 %collective-permute-start.11 = (bf16[2,224,128]{2,1,0:T(8,128)(2,1)}, bf16[2,224,128]{2,1,0:T(8,128)(2,1)}, u32[]{:S(2)}, u32[]{:S(2)}) collective-permute-start(bf16[2,224,128]{2,1,0:T(8,128)(2,1)} %get-tuple-element.37), channel_id=1, source_target_pairs={{0,2},{1,3},{2,4},{3,5},{4,6},{5,7},{6,0},{7,1},{8,10},{9,11},{10,... | collective-permute-start | bytes 344072 | tf_op jit(solution)/shard_map/ppermute | solution.py:228
  116.6 1.4 collective-permute-start.12
  118.0 1.4 collective-permute-start.13
  119.4 0.7 pad_add_fusion.place
  120.1 5.1 %all-gather.3.cloned.1.call-done = bf16[160,96,256]{2,1,0:T(8,128)(2,1)} async-done(((bf16[5,96,256]{2,1,0:T(8,128)(2,1)}), bf16[160,96,256]{2,1,0:T(8,128)(2,1)}) %all-gather.3.cloned.1.call-update) | async-done | bytes 7864336 | tf_op jit(solution)/shard_map/all_gather | solution.py:334
  125.1 4.7 %shard_map.170 = bf16[8,40,384]{2,1,0:T(8,128)(2,1)} custom-call(s32[2]{0:T(128)} %pad_add_fusion.place, bf16[4,2,4,2,48,128]{5,4,3,2,1,0:T(8,128)(2,1)} %copy-done.4, bf16[4,2,4,2,48,128]{5,4,3,2,1,0:T(8,128)(2,1)} %copy-done.7, bf16[32,5,96,256]{3,2,1,0:T(8,128)(2,1)} %bitcast.35), custom_call_target="tpu_custom_call" | custom-call | bytes 8000000 | tf_op jit(solution)/shard_map/pallas_call | solution.py:167
  129.9 0.6 copy-done.10
  130.5 0.1 copy-done.11
  130.5 7.4 %shard_map.171 = (bf16[224,3072]{1,0:T(8,128)(2,1)}, bf16[224,3072]{1,0:T(8,128)(2,1)}) custom-call(s32[1]{0:T(128)} %bitcast.core, bf16[2,224,128]{2,1,0:T(8,128)(2,1)} %get-tuple-element.32.refs_0_, bf16[2,224,128]{2,1,0:T(8,128)(2,1)} %copy-done.10, bf16[2,224,128]{2,1,0:T(8,128)(2,1)} %copy-done.11, bf16[2,224,128]{2,1,0:T(8,128)(2,1)} %copy-done.9, ...), custom_call_target="tpu_custom_call" | custom-call | bytes 25000000 | tf_op jit(solution)/shard_map/pallas_call | solution.py:210
  137.9 1.1 collective-permute-start.14
  139.0 10.5 %all_to_all.15.parts = bf16[8,40,384]{2,1,0:T(8,128)(2,1)S(1)} all-to-all(bf16[8,40,384]{2,1,0:T(8,128)(2,1)S(1)} %copy-done.6), channel_id=1, replica_groups=mesh['dp'=32,'uly'=8] {'uly'}, dimensions={0} | all-to-all | bytes 491520 | tf_op jit(solution)/shard_map/all_to_all | solution.py:368
  149.5 0.8 shard_map.173
  150.2 1.3 copy-done.2
  151.6 2.2 %shard_map.172 = bf16[1,220,3072]{2,1,0:T(8,128)(2,1)} custom-call(bf16[224,3072]{1,0:T(8,128)(2,1)S(1)} %copy-done.2, bf16[224,3072]{1,0:T(8,128)(2,1)S(1)} %collective-permute-done.14.other, bf16[1,220,3072]{2,1,0:T(8,128)(2,1)S(1)} %copy-done.1, f32[1,3072]{1,0:T(1,128)S(1)} %fusion.3.gate), custom_call_target="tpu_custom_call" | custom-call | bytes 6000000 | tf_op jit(solution)/shard_map/pallas_call | solution.py:254
  (47 shorter events, 0.1 us)
Async XLA Ops:
  7.2 32.0 %copy-start = (bf16[256,3072]{1,0:T(8,128)(2,1)S(1)}, bf16[256,3072]{1,0:T(8,128)(2,1)}, u32[]{:S(2)}) copy-start(bf16[256,3072]{1,0:T(8,128)(2,1)} %param.26) | copy-start | bytes 4718596
  7.2 118.0 %all-gather.3.cloned.1.call-start = ((), (), s32[]{:S(2)}) async-start(), calls=%async_computation.3 | async-start | bytes 8110080 | tf_op jit(solution)/shard_map/all_gather | solution.py:334
  7.2 16.7 %collective-permute-start.4 = (bf16[96,256]{1,0:T(8,128)(2,1)}, bf16[96,256]{1,0:T(8,128)(2,1)S(1)}, u32[]{:S(2)}, u32[]{:S(2)}) collective-permute-start(bf16[96,256]{1,0:T(8,128)(2,1)} %bitcast.42), channel_id=1, source_target_pairs={{0,2},{1,3},{2,4},{3,5},{4,6},{5,7},{6,0},{7,1},{8,10},{9,11},{10,... | collective-permute-start | bytes 147464 | tf_op jit(solution)/shard_map/ppermute | solution.py:228
  9.3 14.6 %collective-permute-start.5 = (bf16[96,256]{1,0:T(8,128)(2,1)}, bf16[96,256]{1,0:T(8,128)(2,1)S(1)}, u32[]{:S(2)}, u32[]{:S(2)}) collective-permute-start(bf16[96,256]{1,0:T(8,128)(2,1)} %bitcast.43), channel_id=1, source_target_pairs={{0,4},{1,5},{2,6},{3,7},{4,0},{5,1},{6,2},{7,3},{8,12},{9,13},{10,... | collective-permute-start | bytes 147464 | tf_op jit(solution)/shard_map/ppermute | solution.py:228
  11.8 12.2 %collective-permute-start.6 = (bf16[96,256]{1,0:T(8,128)(2,1)}, bf16[96,256]{1,0:T(8,128)(2,1)S(1)}, u32[]{:S(2)}, u32[]{:S(2)}) collective-permute-start(bf16[96,256]{1,0:T(8,128)(2,1)} %bitcast.44), channel_id=1, source_target_pairs={{0,6},{1,7},{2,0},{3,1},{4,2},{5,3},{6,4},{7,5},{8,14},{9,15},{10,... | collective-permute-start | bytes 147464 | tf_op jit(solution)/shard_map/ppermute | solution.py:228
  12.9 12.2 %collective-permute-start.7 = (bf16[96,256]{1,0:T(8,128)(2,1)}, bf16[96,256]{1,0:T(8,128)(2,1)S(1)}, u32[]{:S(2)}, u32[]{:S(2)}) collective-permute-start(bf16[96,256]{1,0:T(8,128)(2,1)} %bitcast.45), channel_id=1, source_target_pairs={{0,0},{1,32},{2,64},{3,96},{4,128},{5,160},{6,192},{7,224},{8,8},{... | collective-permute-start | bytes 147464 | tf_op jit(solution)/shard_map/ppermute | solution.py:333
  25.1 0.7 copy-start.8
  29.3 7.9 %copy-start.15 = (s32[16]{0:T(128)S(1)}, s32[16]{0:T(128)}, u32[]{:S(2)}) copy-start(s32[16]{0:T(128)} %param.29) | copy-start | bytes 196
  29.3 29.0 %all-to-all-start = ((bf16[8,272,384]{2,1,0:T(8,128)(2,1)}), bf16[8,272,384]{2,1,0:T(8,128)(2,1)}, u32[]{:S(2)}, u32[]{:S(2)}) async-start(bf16[8,272,384]{2,1,0:T(8,128)(2,1)} %get-tuple-element.23), calls=%async_computation | async-start | bytes 3342336 | tf_op jit(solution)/shard_map/all_to_all | solution.py:338
  36.5 3.0 %copy-start.5 = (bf16[256,3072]{1,0:T(8,128)(2,1)S(1)}, bf16[256,3072]{1,0:T(8,128)(2,1)}, u32[]{:S(2)}) copy-start(bf16[256,3072]{1,0:T(8,128)(2,1)} %param.27) | copy-start | bytes 4718596
  58.4 5.2 %copy-start.13 = (f32[16]{0:T(128)S(1)}, f32[16]{0:T(128)}, u32[]{:S(2)}) copy-start(f32[16]{0:T(128)} %param.28) | copy-start | bytes 196
  58.4 27.1 %all-to-all-start.1 = ((bf16[8,272,384]{2,1,0:T(8,128)(2,1)}), bf16[8,272,384]{2,1,0:T(8,128)(2,1)}, u32[]{:S(2)}, u32[]{:S(2)}) async-start(bf16[8,272,384]{2,1,0:T(8,128)(2,1)} %get-tuple-element.29), calls=%async_computation.1 | async-start | bytes 3342336 | tf_op jit(solution)/shard_map/all_to_all | solution.py:357
  85.4 11.1 %copy-start.12 = (bf16[4,2,48,128]{3,2,1,0:T(8,128)(2,1)S(1)}, bf16[4,2,48,128]{3,2,1,0:T(8,128)(2,1)}, u32[]{:S(2)}) copy-start(bf16[4,2,48,128]{3,2,1,0:T(8,128)(2,1)} %get-tuple-element.27) | copy-start | bytes 294916
  96.5 14.6 %copy-start.14 = (bf16[2,224,128]{2,1,0:T(8,128)(2,1)S(1)}, bf16[2,224,128]{2,1,0:T(8,128)(2,1)}, u32[]{:S(2)}) copy-start(bf16[2,224,128]{2,1,0:T(8,128)(2,1)} %get-tuple-element.35) | copy-start | bytes 344068
  97.5 7.5 %collective-permute-start = (bf16[2,4,2,48,128]{4,3,2,1,0:T(8,128)(2,1)S(1)}, bf16[2,4,2,48,128]{4,3,2,1,0:T(8,128)(2,1)S(1)}, u32[]{:S(2)}, u32[]{:S(2)}) collective-permute-start(bf16[2,4,2,48,128]{4,3,2,1,0:T(8,128)(2,1)S(1)} %get-tuple-element.45), channel_id=1, source_target_pairs={{0,2},{1,3},{2,4},{3,5},{4,6},{5,7},{6,0},{7,1},{8,10},{9,11},{10,... | collective-permute-start | bytes 589832 | tf_op jit(solution)/shard_map/ppermute | solution.py:228
  97.9 10.1 %collective-permute-start.1 = (bf16[2,4,2,48,128]{4,3,2,1,0:T(8,128)(2,1)S(1)}, bf16[2,4,2,48,128]{4,3,2,1,0:T(8,128)(2,1)S(1)}, u32[]{:S(2)}, u32[]{:S(2)}) collective-permute-start(bf16[2,4,2,48,128]{4,3,2,1,0:T(8,128)(2,1)S(1)} %get-tuple-element.45), channel_id=1, source_target_pairs={{0,4},{1,5},{2,6},{3,7},{4,0},{5,1},{6,2},{7,3},{8,12},{9,13},{10,... | collective-permute-start | bytes 589832 | tf_op jit(solution)/shard_map/ppermute | solution.py:228
  99.6 9.4 %collective-permute-start.2 = (bf16[2,4,2,48,128]{4,3,2,1,0:T(8,128)(2,1)S(1)}, bf16[2,4,2,48,128]{4,3,2,1,0:T(8,128)(2,1)S(1)}, u32[]{:S(2)}, u32[]{:S(2)}) collective-permute-start(bf16[2,4,2,48,128]{4,3,2,1,0:T(8,128)(2,1)S(1)} %get-tuple-element.45), channel_id=1, source_target_pairs={{0,6},{1,7},{2,0},{3,1},{4,2},{5,3},{6,4},{7,5},{8,14},{9,15},{10,... | collective-permute-start | bytes 589832 | tf_op jit(solution)/shard_map/ppermute | solution.py:228
  109.1 16.0 %copy-start.4 = (bf16[4,2,4,2,48,128]{5,4,3,2,1,0:T(8,128)(2,1)}, bf16[4,2,4,2,48,128]{5,4,3,2,1,0:T(8,128)(2,1)S(1)}, u32[]{:S(2)}) copy-start(bf16[4,2,4,2,48,128]{5,4,3,2,1,0:T(8,128)(2,1)S(1)} %pad_maximum_fusion.own) | copy-start | bytes 2359300
  109.1 8.9 %collective-permute-start.3 = (bf16[4,2,4,2,48,128]{5,4,3,2,1,0:T(8,128)(2,1)S(1)}, bf16[4,2,4,2,48,128]{5,4,3,2,1,0:T(8,128)(2,1)S(1)}, u32[]{:S(2)}, u32[]{:S(2)}) collective-permute-start(bf16[4,2,4,2,48,128]{5,4,3,2,1,0:T(8,128)(2,1)S(1)} %pad_maximum_fusion.own), channel_id=1, source_target_pairs={{0,1},{1,0},{2,3},{3,2},{4,5},{5,4},{6,7},{7,6},{8,9},{9,8},{10,11... | collective-permute-start | bytes 2359304 | tf_op jit(solution)/shard_map/ppermute | solution.py:364
  111.2 5.4 %collective-permute-start.10 = (bf16[2,224,128]{2,1,0:T(8,128)(2,1)S(1)}, bf16[2,224,128]{2,1,0:T(8,128)(2,1)S(1)}, u32[]{:S(2)}, u32[]{:S(2)}) collective-permute-start(bf16[2,224,128]{2,1,0:T(8,128)(2,1)S(1)} %copy-done.14), channel_id=1, source_target_pairs={{0,6},{1,7},{2,0},{3,1},{4,2},{5,3},{6,4},{7,5},{8,14},{9,15},{10,... | collective-permute-start | bytes 344072 | tf_op jit(solution)/shard_map/ppermute | solution.py:228
  113.3 16.5 %collective-permute-start.8 = (bf16[2,224,128]{2,1,0:T(8,128)(2,1)}, bf16[2,224,128]{2,1,0:T(8,128)(2,1)S(1)}, u32[]{:S(2)}, u32[]{:S(2)}) collective-permute-start(bf16[2,224,128]{2,1,0:T(8,128)(2,1)} %get-tuple-element.33), channel_id=1, source_target_pairs={{0,2},{1,3},{2,4},{3,5},{4,6},{5,7},{6,0},{7,1},{8,10},{9,11},{10,... | collective-permute-start | bytes 344072 | tf_op jit(solution)/shard_map/ppermute | solution.py:228
  113.3 16.5 %collective-permute-start.9 = (bf16[2,224,128]{2,1,0:T(8,128)(2,1)}, bf16[2,224,128]{2,1,0:T(8,128)(2,1)S(1)}, u32[]{:S(2)}, u32[]{:S(2)}) collective-permute-start(bf16[2,224,128]{2,1,0:T(8,128)(2,1)} %get-tuple-element.34), channel_id=1, source_target_pairs={{0,4},{1,5},{2,6},{3,7},{4,0},{5,1},{6,2},{7,3},{8,12},{9,13},{10,... | collective-permute-start | bytes 344072 | tf_op jit(solution)/shard_map/ppermute | solution.py:228
  114.5 15.3 %collective-permute-start.11 = (bf16[2,224,128]{2,1,0:T(8,128)(2,1)}, bf16[2,224,128]{2,1,0:T(8,128)(2,1)}, u32[]{:S(2)}, u32[]{:S(2)}) collective-permute-start(bf16[2,224,128]{2,1,0:T(8,128)(2,1)} %get-tuple-element.37), channel_id=1, source_target_pairs={{0,2},{1,3},{2,4},{3,5},{4,6},{5,7},{6,0},{7,1},{8,10},{9,11},{10,... | collective-permute-start | bytes 344072 | tf_op jit(solution)/shard_map/ppermute | solution.py:228
  116.6 13.2 %copy-start.9 = (bf16[2,224,128]{2,1,0:T(8,128)(2,1)}, bf16[2,224,128]{2,1,0:T(8,128)(2,1)S(1)}, u32[]{:S(2)}) copy-start(bf16[2,224,128]{2,1,0:T(8,128)(2,1)S(1)} %collective-permute-done.10.refs_3_) | copy-start | bytes 344068
  116.6 13.3 %collective-permute-start.12 = (bf16[2,224,128]{2,1,0:T(8,128)(2,1)}, bf16[2,224,128]{2,1,0:T(8,128)(2,1)}, u32[]{:S(2)}, u32[]{:S(2)}) collective-permute-start(bf16[2,224,128]{2,1,0:T(8,128)(2,1)} %get-tuple-element.38), channel_id=1, source_target_pairs={{0,4},{1,5},{2,6},{3,7},{4,0},{5,1},{6,2},{7,3},{8,12},{9,13},{10,... | collective-permute-start | bytes 344072 | tf_op jit(solution)/shard_map/ppermute | solution.py:228
  118.0 7.1 %copy-start.7 = (bf16[4,2,4,2,48,128]{5,4,3,2,1,0:T(8,128)(2,1)}, bf16[4,2,4,2,48,128]{5,4,3,2,1,0:T(8,128)(2,1)S(1)}, u32[]{:S(2)}) copy-start(bf16[4,2,4,2,48,128]{5,4,3,2,1,0:T(8,128)(2,1)S(1)} %collective-permute-done.3.other) | copy-start | bytes 2359300
  118.0 11.8 %collective-permute-start.13 = (bf16[2,224,128]{2,1,0:T(8,128)(2,1)}, bf16[2,224,128]{2,1,0:T(8,128)(2,1)}, u32[]{:S(2)}, u32[]{:S(2)}) collective-permute-start(bf16[2,224,128]{2,1,0:T(8,128)(2,1)} %get-tuple-element.39), channel_id=1, source_target_pairs={{0,6},{1,7},{2,0},{3,1},{4,2},{5,3},{6,4},{7,5},{8,14},{9,15},{10,... | collective-permute-start | bytes 344072 | tf_op jit(solution)/shard_map/ppermute | solution.py:228
  129.8 0.6 copy-start.10
  129.8 0.7 copy-start.11
  130.5 8.5 %copy-start.6 = (bf16[8,40,384]{2,1,0:T(8,128)(2,1)S(1)}, bf16[8,40,384]{2,1,0:T(8,128)(2,1)}, u32[]{:S(2)}) copy-start(bf16[8,40,384]{2,1,0:T(8,128)(2,1)} %shard_map.170) | copy-start | bytes 737284
  130.5 19.0 %copy-start.3 = (bf16[1,40,3072]{2,1,0:T(8,128)(2,1)S(1)}, bf16[1,40,3072]{2,1,0:T(8,128)(2,1)}, u32[]{:S(2)}) copy-start(bf16[1,40,3072]{2,1,0:T(8,128)(2,1)} %x.3) | copy-start | bytes 737284
  130.5 19.7 %copy-start.1 = (bf16[1,220,3072]{2,1,0:T(8,128)(2,1)S(1)}, bf16[1,220,3072]{2,1,0:T(8,128)(2,1)}, u32[]{:S(2)}) copy-start(bf16[1,220,3072]{2,1,0:T(8,128)(2,1)} %x.2) | copy-start | bytes 4055044
  137.9 12.4 %collective-permute-start.14 = (bf16[224,3072]{1,0:T(8,128)(2,1)}, bf16[224,3072]{1,0:T(8,128)(2,1)S(1)}, u32[]{:S(2)}, u32[]{:S(2)}) collective-permute-start(bf16[224,3072]{1,0:T(8,128)(2,1)} %get-tuple-element.41), channel_id=1, source_target_pairs={{0,1},{1,0},{2,3},{3,2},{4,5},{5,4},{6,7},{7,6},{8,9},{9,8},{10,11... | collective-permute-start | bytes 4128776 | tf_op jit(solution)/shard_map/ppermute | solution.py:370
  150.2 1.3 copy-start.2
Sparse Core Ops, SparseCore 0:
  26.0 99.1 all-gather.2

commit v2 on v1

--- a/solution.py
+++ b/solution.py
@@ -20,6 +20,7 @@
 AROWS = 48
 ROWS = VROWS + AROWS
 KEYS = GROUPS * ROWS
+MESSAGE = 2 * VROWS + GROUPS * AROWS
 LOG2E = math.log2(math.e)
 SCALE2 = LOG2E / math.sqrt(HEAD_DIM)
 OUTSIDE = 1e30
@@ -69,7 +70,7 @@
 
 
 def attend_kernel(chip, scalars, key_rows, query, keys, values, *refs):
-    outs, out_audio, values_ones = refs[:-2], refs[-2], refs[-1]
+    outs, values_ones = refs[:-1], refs[-1]
     step = pl.program_id(0)
     first = lax.rem(chip[0] + step, XS) * 2
 
@@ -104,18 +105,18 @@
         jnp.concatenate([query[side, VROWS:, :] for side in range(2)], axis=0),
         jnp.concatenate(times, axis=0),
     )
-    for side in range(2):
-        out_audio[first // 2, side] = audio[side * AROWS : (side + 1) * AROWS]
     for dx, out in enumerate(outs):
+        low = pl.multiple_of(2 * VROWS + first * AROWS, 16)
+        out[pl.ds(low, 2 * AROWS), :] = audio
 
         @pl.when(step == dx)
         def _(out=out):
             for side in range(2):
-                out[side] = video[side]
+                out[side * VROWS : (side + 1) * VROWS, :] = video[side]
 
 
 def attend(chip, scalars, key_rows, qkv):
-    video = jax.ShapeDtypeStruct((2, VROWS, HEAD_DIM), jnp.bfloat16)
+    message = jax.ShapeDtypeStruct((MESSAGE, HEAD_DIM), jnp.bfloat16)
     return pl.pallas_call(
         attend_kernel,
         grid_spec=pltpu.PrefetchScalarGridSpec(
@@ -127,73 +128,59 @@
                 pl.BlockSpec((GROUPS, ROWS, HEAD_DIM), lambda i, c, s: (0, 0, 1)),
                 pl.BlockSpec((GROUPS, ROWS, HEAD_DIM), lambda i, c, s: (0, 0, 2)),
             ],
-            out_specs=[pl.BlockSpec((2, VROWS, HEAD_DIM), lambda i, c, s: (0, 0, 0))] * XS
-            + [pl.BlockSpec((XS, 2, AROWS, HEAD_DIM), lambda i, c, s: (0, 0, 0, 0))],
+            out_specs=[pl.BlockSpec((MESSAGE, HEAD_DIM), lambda i, c, s: (0, 0))] * XS,
             scratch_shapes=[pltpu.VMEM((KEYS, 2 * HEAD_DIM), jnp.bfloat16)],
         ),
-        out_shape=[video] * XS
-        + [jax.ShapeDtypeStruct((XS, 2, AROWS, HEAD_DIM), jnp.bfloat16)],
+        out_shape=[message] * XS,
         compiler_params=pltpu.CompilerParams(vmem_limit_bytes=VMEM),
         cost_estimate=pl.CostEstimate(flops=0, bytes_accessed=1_000_000, transcendentals=0),
     )(chip, scalars, key_rows, qkv, qkv, qkv)
 
 
-def audio_kernel(place, own, other, weight, out, left):
-    chip, core = place[0], place[1]
-    for half, source in enumerate((own, other)):
-        side = core if half == 0 else 1 - core
-        for dx in range(XS):
-            group = lax.rem(chip - dx + XS, XS) * 2 + side
-            for head in range(2):
-                low = pl.multiple_of(group * 256 + head * HEAD_DIM, HEAD_DIM)
-                left[:, pl.ds(low, HEAD_DIM)] = source[dx, head].reshape(
-                    GROUPS * AROWS, HEAD_DIM
-                )
+def audio_kernel(place, *refs):
+    sources, weight, out, left = refs[: 2 * XS], *refs[2 * XS :]
+    for number, source in enumerate(sources):
+        head, dx = divmod(number, XS)
+        low = lax.rem(place[0] - dx + XS, XS) * 256 + head * HEAD_DIM
+        left[:, pl.ds(pl.multiple_of(low, HEAD_DIM), HEAD_DIM)] = source[2 * VROWS :, :]
     columns = out.shape[2]
-    blocks = weight.shape[0] // GROUPS
-    rows = [
-        weight[group * blocks : (group + 1) * blocks, 0].reshape(columns, 256)
-        for group in range(GROUPS)
-    ]
+    rows = [weight[x * ZS : (x + 1) * ZS, 0].reshape(columns, 256) for x in range(XS)]
     total = inner(left[...], jnp.concatenate(rows, axis=1))
     for device in range(GROUPS):
         out[device] = total[device * AROWS : device * AROWS + AUD].astype(jnp.bfloat16)
 
 
-def project_audio(place, own, other, weights):
+def project_audio(place, sources, weights):
     blocks, slots, width, _ = weights.shape
-    whole = pl.BlockSpec(own.shape, lambda n, p: (0,) * own.ndim)
-    out = (GROUPS, AUD, blocks // GROUPS * width)
+    out = (GROUPS, AUD, ZS * width)
     return pl.pallas_call(
         audio_kernel,
         grid_spec=pltpu.PrefetchScalarGridSpec(
             num_scalar_prefetch=1,
             grid=(1,),
-            in_specs=[
-                whole,
-                whole,
-                pl.BlockSpec((blocks, 1, width, 256), lambda n, p: (0, slots - 1, 0, 0)),
-            ],
+            in_specs=[pl.BlockSpec((MESSAGE, HEAD_DIM), lambda n, p: (0, 0))] * (2 * XS)
+            + [pl.BlockSpec((blocks, 1, width, 256), lambda n, p: (0, slots - 1, 0, 0))],
             out_specs=pl.BlockSpec(out, lambda n, p: (0, 0, 0)),
-            scratch_shapes=[pltpu.VMEM((GROUPS * AROWS, GROUPS * 256), jnp.bfloat16)],
+            scratch_shapes=[pltpu.VMEM((GROUPS * AROWS, XS * 256), jnp.bfloat16)],
         ),
         out_shape=jax.ShapeDtypeStruct(out, jnp.bfloat16),
         compiler_params=pltpu.CompilerParams(vmem_limit_bytes=VMEM),
         cost_estimate=pl.CostEstimate(flops=0, bytes_accessed=8_000_000, transcendentals=0),
-    )(place, own, other, weights)
-
-
-def project_kernel(core, *refs):
+    )(place, *sources, weights)
+
+
+def project_kernel(place, *refs):
     sources, weight, own, other, left = refs[: 2 * XS], *refs[2 * XS :]
 
     @pl.when(pl.program_id(0) == 0)
     def _():
         for half in range(2):
-            side = core[0] if half == 0 else 1 - core[0]
+            side = place[1] if half == 0 else 1 - place[1]
+            low = pl.multiple_of(side * VROWS, 32)
             for number, source in enumerate(sources):
                 head, dx = divmod(number, XS)
                 lanes = pl.ds(dx * 256 + head * HEAD_DIM, HEAD_DIM)
-                left[half * VROWS : (half + 1) * VROWS, lanes] = source[side]
+                left[half * VROWS : (half + 1) * VROWS, lanes] = source[pl.ds(low, VROWS), :]
 
     columns = own.shape[1]
     rows = [weight[:, dx].reshape(columns, 256) for dx in range(XS)]
@@ -202,25 +189,27 @@
     other[...] = total[VROWS:].astype(jnp.bfloat16)
 
 
-def project(core, sources, weights):
-    blocks, _, width, _ = weights.shape
-    step = ZS
-    out = pl.BlockSpec((VROWS, step * width), lambda n, c: (0, n))
-    shape = jax.ShapeDtypeStruct((VROWS, blocks * width), jnp.bfloat16)
+def project(place, sources, weights):
+    width = weights.shape[2]
+    step, count = ZS, YS
+    out = pl.BlockSpec((VROWS, step * width), lambda n, p: (0, n))
+    shape = jax.ShapeDtypeStruct((VROWS, count * step * width), jnp.bfloat16)
     return pl.pallas_call(
         project_kernel,
         grid_spec=pltpu.PrefetchScalarGridSpec(
             num_scalar_prefetch=1,
-            grid=(blocks // step,),
-            in_specs=[pl.BlockSpec((2, VROWS, HEAD_DIM), lambda n, c: (0, 0, 0))] * (2 * XS)
-            + [pl.BlockSpec((step, XS, width, 256), lambda n, c: (n, 0, 0, 0))],
+            grid=(count,),
+            in_specs=[pl.BlockSpec((MESSAGE, HEAD_DIM), lambda n, p: (0, 0))] * (2 * XS)
+            + [pl.BlockSpec((step, XS, width, 256), lambda n, p: (n, 0, 0, 0))],
             out_specs=[out, out],
             scratch_shapes=[pltpu.VMEM((2 * VROWS, XS * 256), jnp.bfloat16)],
         ),
         out_shape=[shape, shape],
         compiler_params=pltpu.CompilerParams(vmem_limit_bytes=VMEM),
-        cost_estimate=pl.CostEstimate(flops=0, bytes_accessed=25_000_000, transcendentals=0),
-    )(core, *sources, weights)
+        cost_estimate=pl.CostEstimate(
+            flops=0, bytes_accessed=2_000_000 * count, transcendentals=0
+        ),
+    )(place, *sources, weights)
 
 
 def along(array, axis, shift):
@@ -263,7 +252,11 @@
 
 
 def place_kernel(parts, x, gate, out):
-    total = jnp.concatenate([parts[i] for i in range(GROUPS)], axis=1).astype(jnp.float32)
+    quarters = []
+    for chip in range(XS):
+        pair = parts[2 * chip].astype(jnp.float32) + parts[2 * chip + 1].astype(jnp.float32)
+        quarters.append(pair)
+    total = jnp.concatenate(quarters, axis=1)
     out[0] = (x[0].astype(jnp.float32) + gate[...] * total).astype(jnp.bfloat16)
 
 
@@ -323,17 +316,18 @@
     shifts = (1, 2, -1)
 
     block = out_video_w.T
-    slots = [block] + [along(block, "x", shift) for shift in shifts]
-    own_blocks = YS * ZS // GROUPS
+    near = [along(block, "x", shift) for shift in shifts]
     moves = []
-    for column in range(YS * ZS):
+    for over in range(YS * ZS):
+        row, column = divmod(over, ZS)
         for group in range(GROUPS):
-            over = group // 2 * ZS + group % 2 * own_blocks + column % own_blocks
-            moves.append((column * GROUPS + group, over * GROUPS + column // own_blocks))
-    slots.append(lax.ppermute(out_audio_w.T, ("dp", "uly"), moves))
-    weights = lax.all_gather(jnp.stack(slots), "dp", axis=0, tiled=False)
-
+            target = (group // 2 * ZS + column) * GROUPS + row * 2 + group % 2
+            moves.append((over * GROUPS + group, target))
+    block_a = lax.ppermute(out_audio_w.T, ("dp", "uly"), moves)
     packed = pack((q_video, k_video, v_video, q_audio, k_audio, v_audio))
+    block, *near = lax.optimization_barrier((block, *near, packed[0]))[:-1]
+    weights = lax.all_gather(jnp.stack([block, *near, block_a]), "dp", axis=0, tiled=False)
+
     qkv = [None, None]
     qkv[0] = lax.all_to_all(packed[0], "uly", split_axis=0, concat_axis=0, tiled=True)
 
@@ -349,24 +343,24 @@
 
     def attention(head, qkv):
         scalars = jnp.stack([slopes[position * own_heads + head], offset])
-        *video, audio = attend(chip[None], scalars, key_rows, qkv)
-        sent = [along(array, "x", dx) if dx else array for dx, array in enumerate(video)]
-        return sent, audio, video[0]
+        messages = attend(chip[None], scalars, key_rows, qkv)
+        sent = [along(array, "x", dx) if dx else array for dx, array in enumerate(messages)]
+        return sent, messages[0]
 
     first, gate_v, gate_a, key_rows = lax.optimization_barrier((qkv[0], gate_v, gate_a, key_rows))
     qkv[1] = lax.all_to_all(
         after(packed[1], first), "uly", split_axis=0, concat_axis=0, tiled=True
     )
-    sent0, audio0, done = attention(0, first)
-    sent1, audio1, _ = attention(1, after(qkv[1], done))
-    audio = jnp.stack([audio0, audio1])
-    audio = jnp.stack([audio] + [along(audio, "x", shift) for shift in shifts])
-    other_audio = lax.ppermute(audio, "uly", swap)
-    parts = project_audio(jnp.stack([chip, core]), audio, other_audio, weights)
+    sent0, done = attention(0, first)
+    sent1, _ = attention(1, after(qkv[1], done))
+    place = jnp.stack([chip, core])
     sources = sent0 + sent1
-    sources[0] = after(sources[0], parts)
+    parts = project_audio(place, sources, weights)
+    early = list(sources)
+    early[0] = after(sources[0], parts)
     parts = lax.all_to_all(parts, "uly", split_axis=0, concat_axis=0, tiled=True)
-    own, other = project(core[None], sources, weights)
+    own, other = project(place, early, weights)
+    other, parts = lax.optimization_barrier((other, parts))
     received = lax.ppermute(other, "uly", swap)
     out_audio = finish_audio(parts, x_audio, gate_a)
     return finish_video(own, received, x_video, gate_v), out_audio

time: 161 us -> 155 us (0.963)
  blocking collectives: 10.5 us -> 0 us
  waiting for transfers between devices: 41.2 us -> 49.2 us
  starting transfers between devices: 42.5 us -> 36.7 us
  local copies, waits for them, and re-layouts: 4.14 us -> 5.93 us
    all_gather x1, waiting for transfers between devices: 5.06 us -> 17.8 us  [shards(): lax.all_gather(jnp.stack([block, *near, block_a]), 'dp', axis=0, tiled=Fa...]
    ppermute x2 -> x1, starting transfers between devices: 12.2 us -> 1.58 us  [shards(): block_a = lax.ppermute(out_audio_w.T, ('dp', 'uly'), moves)]
    all_to_all x1 -> x0, blocking collectives: 10.5 us -> none  [shards(): lax.all_to_all(parts, 'uly', split_axis=0, concat_axis=0, tiled=True)]
    all_to_all x0 -> x1, starting transfers between devices: none -> 5.34 us  [shards(): lax.all_to_all(parts, 'uly', split_axis=0, concat_axis=0, tiled=True)]
    all_to_all x1, waiting for transfers between devices: 8.51 us -> 3.39 us  [shards(): lax.all_to_all(after(packed[1], first), 'uly', split_axis=0, concat_axis=...]
    ppermute x12 -> x9, starting transfers between devices: 16.8 us -> 12.4 us  [along(): lax.ppermute(array, 'uly', [(i, (i + 2 * shift) % GROUPS) for i in range(...]
    all_to_all x1, starting transfers between devices: 7.14 us -> 11.4 us  [shards(): lax.all_to_all(packed[0], 'uly', split_axis=0, concat_axis=0, tiled=True)]
    unnamed x36, local copies, waits for them, and re-layouts: 3.54 us -> 5.31 us
  transfers between devices with their start and end apart: 18 -> 15, of which waited for: 7 -> 8; matrix products, arithmetic and copies ran while one was open for 4% -> 3% of each run, Pallas kernels for 19% -> 23%
where the time goes in v2:
time: 155 us; the launch traced here: 154 us
  waiting for transfers between devices  49.2 us (32%)
  Pallas kernels  41.3 us (27%)
  starting transfers between devices  36.7 us (24%)
  between operations  16.2 us (10%)
  local copies, waits for them, and re-layouts  5.93 us (4%)
  other arithmetic  3.99 us (3%)
    pallas_call x2, Pallas kernels, attend(): pl.pallas_call(attend_kernel, grid_spec=pltpu.PrefetchScalarGridSpec(num_...  22.2 us
    all_gather x1, waiting for transfers between devices, shards(): lax.all_gather(jnp.stack([block, *near, block_a]), 'dp', axis=0, tiled=Fa...  17.8 us
    all_to_all x1, waiting for transfers between devices, shards(): lax.all_to_all(packed[0], 'uly', split_axis=0, concat_axis=0, tiled=True)  16.7 us
    ppermute x9, starting transfers between devices, along(): lax.ppermute(array, 'uly', [(i, (i + 2 * shift) % GROUPS) for i in range(...  12.4 us
    all_to_all x1, starting transfers between devices, shards(): lax.all_to_all(packed[0], 'uly', split_axis=0, concat_axis=0, tiled=True)  11.4 us
    ppermute x9, waiting for transfers between devices, along(): lax.ppermute(array, 'uly', [(i, (i + 2 * shift) % GROUPS) for i in range(...  9.18 us
    pallas_call x1, Pallas kernels, project(): pl.pallas_call(project_kernel, grid_spec=pltpu.PrefetchScalarGridSpec(num...  8.27 us
    all_to_all x1, starting transfers between devices, shards(): lax.all_to_all(parts, 'uly', split_axis=0, concat_axis=0, tiled=True)  5.34 us
  transfers between devices with their start and end apart: 15, of which 8 were waited for; matrix products, arithmetic and copies ran while one was open for 3% of the time, Pallas kernels for 23%

profile of v2, /device:TPU:1, one launch (start us, length us, event | category | flops | bytes accessed | tf_op | source)
XLA Modules:
  0.0 153.9 jit_solution(815750850866921565)
XLA Ops:
  7.2 0.0 copy-start
  7.2 0.0 all-gather.3.cloned.1.call-start
  7.2 3.4 %collective-permute-start.8 = (bf16[96,256]{1,0:T(8,128)(2,1)}, bf16[96,256]{1,0:T(8,128)(2,1)S(1)}, u32[]{:S(2)}, u32[]{:S(2)}) collective-permute-start(bf16[96,256]{1,0:T(8,128)(2,1)} %bitcast.29), channel_id=1, source_target_pairs={{0,6},{1,7},{2,0},{3,1},{4,2},{5,3},{6,4},{7,5},{8,14},{9,15},{10,... | collective-permute-start | bytes 147464 | tf_op jit(solution)/shard_map/ppermute | solution.py:217
  10.6 0.5 collective-permute-start.7
  11.1 0.6 collective-permute-start.6
  11.7 1.6 %collective-permute-start.9 = (bf16[96,256]{1,0:T(8,128)(2,1)}, bf16[96,256]{1,0:T(8,128)(2,1)S(1)}, u32[]{:S(2)}, u32[]{:S(2)}) collective-permute-start(bf16[96,256]{1,0:T(8,128)(2,1)} %bitcast.33), channel_id=1, source_target_pairs={{0,0},{1,1},{2,64},{3,65},{4,128},{5,129},{6,192},{7,193},{8,8},{9... | collective-permute-start | bytes 147464 | tf_op jit(solution)/shard_map/ppermute | solution.py:326
  13.3 3.4 %shard_map.167 = (bf16[8,272,384]{2,1,0:T(8,128)(2,1)}, bf16[8,272,384]{2,1,0:T(8,128)(2,1)}) custom-call(bf16[1,220,2048]{2,1,0:T(8,128)(2,1)} %refs_0_.1, bf16[1,220,2048]{2,1,0:T(8,128)(2,1)} %refs_1_.1, bf16[1,220,2048]{2,1,0:T(8,128)(2,1)} %refs_2_.1, bf16[1,40,2048]{2,1,0:T(8,128)(2,1)} %refs_3_.1, bf16[1,40,2048]{2,1,0:T(8,128)(2,1)} %refs_4_.1, ...), custom_call_target="tpu_custom_call" | custom-call | bytes 1000000 | tf_op jit(solution)/shard_map/pallas_call | solution.py:55
  16.9 0.0 copy-start.12
  16.9 0.7 copy-done.12
  17.6 0.0 all-gather.3.cloned.1.call-update
  17.6 11.4 %all-to-all-start = ((bf16[8,272,384]{2,1,0:T(8,128)(2,1)}), bf16[8,272,384]{2,1,0:T(8,128)(2,1)S(1)}, u32[]{:S(2)}, u32[]{:S(2)}) async-start(bf16[8,272,384]{2,1,0:T(8,128)(2,1)} %get-tuple-element.27), calls=%async_computation | async-start | bytes 3342336 | tf_op jit(solution)/shard_map/all_to_all | solution.py:332
  29.6 0.7 fusion
  31.6 0.0 copy-start.5
  31.6 0.1 sine_convert_fusion
  31.7 0.3 fusion.3.gate
  32.0 1.0 copy-done.5
  33.0 0.3 fusion.2.gate
  33.3 0.1 or_select_fusion
  33.4 0.6 pad_maximum_fusion.key_rows
  34.0 16.7 %all-to-all-done.query.keys.values = bf16[8,272,384]{2,1,0:T(8,128)(2,1)S(1)} async-done(((bf16[8,272,384]{2,1,0:T(8,128)(2,1)}), bf16[8,272,384]{2,1,0:T(8,128)(2,1)S(1)}, u32[]{:S(2)}, u32[]{:S(2)}) %all-to-all-start) | async-done | bytes 1671200 | tf_op jit(solution)/shard_map/all_to_all | solution.py:332
  50.7 1.3 copy-done.4
  52.0 5.1 %all-to-all-start.1 = ((bf16[8,272,384]{2,1,0:T(8,128)(2,1)}), bf16[8,272,384]{2,1,0:T(8,128)(2,1)}, u32[]{:S(2)}, u32[]{:S(2)}) async-start(bf16[8,272,384]{2,1,0:T(8,128)(2,1)} %get-tuple-element.35), calls=%async_computation.1 | async-start | bytes 3342336 | tf_op jit(solution)/shard_map/all_to_all | solution.py:351
  57.1 0.6 fusion.1
  57.7 1.9 %pad_maximum_fusion.1 = (f32[2]{0:T(128)}, f32[2]{0:T(128)}) fusion(f32[1]{0:T(128)} %get-tuple-element.53, f32[1]{0:T(128)} %bitcast.3, f32[1]{0:T(128)} %get-tuple-element.52), kind=kLoop, calls=%fused_computation.20 | loop fusion | flops 4 | bytes 28 | tf_op jit(solution)/shard_map/stack | solution.py:345
  59.6 11.0 %shard_map.168 = (bf16[832,128]{1,0:T(8,128)(2,1)}, bf16[832,128]{1,0:T(8,128)(2,1)}, bf16[832,128]{1,0:T(8,128)(2,1)}, bf16[832,128]{1,0:T(8,128)(2,1)}) custom-call(s32[1]{0:T(128)} %bitcast.chip, f32[2]{0:T(128)} %get-tuple-element.54.scalars, f32[2,2176]{1,0:T(2,128)} %pad_maximum_fusion.key_rows, bf16[8,272,384]{2,1,0:T(8,128)(2,1)} %copy-done.4, ...), custom_call_target="tpu_custom_call" | custom-call | bytes 1000000 | tf_op jit(solution)/shard_map/pallas_call | solution.py:120
  70.6 1.4 collective-permute-start
  72.0 2.4 %collective-permute-start.1 = (bf16[832,128]{1,0:T(8,128)(2,1)}, bf16[832,128]{1,0:T(8,128)(2,1)S(1)}, u32[]{:S(2)}, u32[]{:S(2)}) collective-permute-start(bf16[832,128]{1,0:T(8,128)(2,1)} %get-tuple-element.32), channel_id=1, source_target_pairs={{0,4},{1,5},{2,6},{3,7},{4,0},{5,1},{6,2},{7,3},{8,12},{9,13},{10,... | collective-permute-start | bytes 638984 | tf_op jit(solution)/shard_map/ppermute | solution.py:217
  74.4 1.2 collective-permute-start.2
  75.6 3.4 %all-to-all-done.1.query.keys.values = bf16[8,272,384]{2,1,0:T(8,128)(2,1)} async-done(((bf16[8,272,384]{2,1,0:T(8,128)(2,1)}), bf16[8,272,384]{2,1,0:T(8,128)(2,1)}, u32[]{:S(2)}, u32[]{:S(2)}) %all-to-all-start.1) | async-done | bytes 1671200 | tf_op jit(solution)/shard_map/all_to_all | solution.py:351
  79.0 11.1 %shard_map.169 = (bf16[832,128]{1,0:T(8,128)(2,1)}, bf16[832,128]{1,0:T(8,128)(2,1)}, bf16[832,128]{1,0:T(8,128)(2,1)}, bf16[832,128]{1,0:T(8,128)(2,1)}) custom-call(s32[1]{0:T(128)} %bitcast.chip, f32[2]{0:T(128)} %get-tuple-element.55.scalars, f32[2,2176]{1,0:T(2,128)} %pad_maximum_fusion.key_rows, bf16[8,272,384]{2,1,0:T(8,128)(2,1)} %all-to-all-done.1.query.keys.values, ...), custom_call_target="tpu_custom_call" | custom-call | bytes 1000000 | tf_op jit(solution)/shard_map/pallas_call | solution.py:120
  90.2 0.3 collective-permute-start.3
  90.5 1.7 %collective-permute-start.4 = (bf16[832,128]{1,0:T(8,128)(2,1)}, bf16[832,128]{1,0:T(8,128)(2,1)S(1)}, u32[]{:S(2)}, u32[]{:S(2)}) collective-permute-start(bf16[832,128]{1,0:T(8,128)(2,1)} %get-tuple-element.39), channel_id=1, source_target_pairs={{0,4},{1,5},{2,6},{3,7},{4,0},{5,1},{6,2},{7,3},{8,12},{9,13},{10,... | collective-permute-start | bytes 638984 | tf_op jit(solution)/shard_map/ppermute | solution.py:217
  92.2 0.9 collective-permute-start.5
  93.1 0.6 pad_add_fusion.place
  93.8 4.1 %collective-permute-done.3.refs_5_ = bf16[832,128]{1,0:T(8,128)(2,1)S(1)} collective-permute-done((bf16[832,128]{1,0:T(8,128)(2,1)}, bf16[832,128]{1,0:T(8,128)(2,1)S(1)}, u32[]{:S(2)}, u32[]{:S(2)}) %collective-permute-start.3) | collective-permute-done | bytes 213024 | tf_op jit(solution)/shard_map/ppermute | solution.py:217
  97.8 3.0 %collective-permute-done.4.refs_6_ = bf16[832,128]{1,0:T(8,128)(2,1)S(1)} collective-permute-done((bf16[832,128]{1,0:T(8,128)(2,1)}, bf16[832,128]{1,0:T(8,128)(2,1)S(1)}, u32[]{:S(2)}, u32[]{:S(2)}) %collective-permute-start.4) | collective-permute-done | bytes 213024 | tf_op jit(solution)/shard_map/ppermute | solution.py:217
  100.8 2.1 %collective-permute-done.5.refs_7_ = bf16[832,128]{1,0:T(8,128)(2,1)S(1)} collective-permute-done((bf16[832,128]{1,0:T(8,128)(2,1)}, bf16[832,128]{1,0:T(8,128)(2,1)S(1)}, u32[]{:S(2)}, u32[]{:S(2)}) %collective-permute-start.5) | collective-permute-done | bytes 213024 | tf_op jit(solution)/shard_map/ppermute | solution.py:217
  102.9 17.8 %all-gather.3.cloned.1.call-done = bf16[160,96,256]{2,1,0:T(8,128)(2,1)} async-done(((bf16[5,96,256]{2,1,0:T(8,128)(2,1)}), bf16[160,96,256]{2,1,0:T(8,128)(2,1)}) %all-gather.3.cloned.1.call-update) | async-done | bytes 7864336 | tf_op jit(solution)/shard_map/all_gather | solution.py:329
  120.8 4.4 %shard_map.170 = bf16[8,40,768]{2,1,0:T(8,128)(2,1)} custom-call(s32[2]{0:T(128)} %pad_add_fusion.place, bf16[832,128]{1,0:T(8,128)(2,1)} %get-tuple-element.45.refs_0_, bf16[832,128]{1,0:T(8,128)(2,1)} %copy-done.6, bf16[832,128]{1,0:T(8,128)(2,1)} %copy-done.7, bf16[832,128]{1,0:T(8,128)(2,1)} %copy-done.8, bf16[832,128]{1,0:T(8,128)(2,1)} %get-tuple-element.37.refs_4_, ...), custom_call_target="tpu_custom_call" | custom-call | bytes 8000000 | tf_op jit(solution)/shard_map/pallas_call | solution.py:156
  125.2 5.3 %all-to-all-start.2 = ((bf16[8,40,768]{2,1,0:T(8,128)(2,1)}), bf16[8,40,768]{2,1,0:T(8,128)(2,1)S(1)}, u32[]{:S(2)}, u32[]{:S(2)}) async-start(bf16[8,40,768]{2,1,0:T(8,128)(2,1)} %shard_map.170), calls=%async_computation.2 | async-start | bytes 983040 | tf_op jit(solution)/shard_map/all_to_all | solution.py:361
  130.6 8.3 %shard_map.171 = (bf16[224,3072]{1,0:T(8,128)(2,1)}, bf16[224,3072]{1,0:T(8,128)(2,1)}) custom-call(s32[2]{0:T(128)} %pad_add_fusion.place, bf16[832,128]{1,0:T(8,128)(2,1)} %get-tuple-element.45.refs_0_, bf16[832,128]{1,0:T(8,128)(2,1)} %copy-done.6, bf16[832,128]{1,0:T(8,128)(2,1)} %copy-done.7, bf16[832,128]{1,0:T(8,128)(2,1)} %copy-done.8, ...), custom_call_target="tpu_custom_call" | custom-call | bytes 8000000 | tf_op jit(solution)/shard_map/pallas_call | solution.py:197
  138.8 0.9 all-to-all-done.2.parts
  139.7 0.9 collective-permute-start.10
  140.6 0.9 copy-done.3
  141.5 0.8 shard_map.173
  142.3 1.2 collective-permute-done.10.other
  143.5 1.3 copy-done.2
  144.9 2.2 %shard_map.172 = bf16[1,220,3072]{2,1,0:T(8,128)(2,1)} custom-call(bf16[224,3072]{1,0:T(8,128)(2,1)S(1)} %copy-done.2, bf16[224,3072]{1,0:T(8,128)(2,1)S(1)} %collective-permute-done.10.other, bf16[1,220,3072]{2,1,0:T(8,128)(2,1)S(1)} %copy-done.1, f32[1,3072]{1,0:T(1,128)S(1)} %fusion.2.gate), custom_call_target="tpu_custom_call" | custom-call | bytes 6000000 | tf_op jit(solution)/shard_map/pallas_call | solution.py:243
  (38 shorter events, 0.1 us)
Async XLA Ops:
  7.2 24.5 %copy-start = (bf16[256,3072]{1,0:T(8,128)(2,1)S(1)}, bf16[256,3072]{1,0:T(8,128)(2,1)}, u32[]{:S(2)}) copy-start(bf16[256,3072]{1,0:T(8,128)(2,1)} %param.27) | copy-start | bytes 4718596
  7.2 113.6 %all-gather.3.cloned.1.call-start = ((), (), s32[]{:S(2)}) async-start(), calls=%async_computation.3 | async-start | bytes 8110080 | tf_op jit(solution)/shard_map/all_gather | solution.py:329
  7.2 9.5 %collective-permute-start.8 = (bf16[96,256]{1,0:T(8,128)(2,1)}, bf16[96,256]{1,0:T(8,128)(2,1)S(1)}, u32[]{:S(2)}, u32[]{:S(2)}) collective-permute-start(bf16[96,256]{1,0:T(8,128)(2,1)} %bitcast.29), channel_id=1, source_target_pairs={{0,6},{1,7},{2,0},{3,1},{4,2},{5,3},{6,4},{7,5},{8,14},{9,15},{10,... | collective-permute-start | bytes 147464 | tf_op jit(solution)/shard_map/ppermute | solution.py:217
  10.6 6.2 %collective-permute-start.7 = (bf16[96,256]{1,0:T(8,128)(2,1)}, bf16[96,256]{1,0:T(8,128)(2,1)S(1)}, u32[]{:S(2)}, u32[]{:S(2)}) collective-permute-start(bf16[96,256]{1,0:T(8,128)(2,1)} %bitcast.30), channel_id=1, source_target_pairs={{0,4},{1,5},{2,6},{3,7},{4,0},{5,1},{6,2},{7,3},{8,12},{9,13},{10,... | collective-permute-start | bytes 147464 | tf_op jit(solution)/shard_map/ppermute | solution.py:217
  11.1 5.7 %collective-permute-start.6 = (bf16[96,256]{1,0:T(8,128)(2,1)}, bf16[96,256]{1,0:T(8,128)(2,1)S(1)}, u32[]{:S(2)}, u32[]{:S(2)}) collective-permute-start(bf16[96,256]{1,0:T(8,128)(2,1)} %bitcast.31), channel_id=1, source_target_pairs={{0,2},{1,3},{2,4},{3,5},{4,6},{5,7},{6,0},{7,1},{8,10},{9,11},{10,... | collective-permute-start | bytes 147464 | tf_op jit(solution)/shard_map/ppermute | solution.py:217
  11.7 5.1 %copy-start.13 = (bf16[256,96]{0,1:T(8,128)(2,1)S(1)}, bf16[256,96]{0,1:T(8,128)(2,1)}, u32[]{:S(2)}) copy-start(bf16[256,96]{0,1:T(8,128)(2,1)} %param.24) | copy-start | bytes 147460
  11.7 5.1 %collective-permute-start.9 = (bf16[96,256]{1,0:T(8,128)(2,1)}, bf16[96,256]{1,0:T(8,128)(2,1)S(1)}, u32[]{:S(2)}, u32[]{:S(2)}) collective-permute-start(bf16[96,256]{1,0:T(8,128)(2,1)} %bitcast.33), channel_id=1, source_target_pairs={{0,0},{1,1},{2,64},{3,65},{4,128},{5,129},{6,192},{7,193},{8,8},{9... | collective-permute-start | bytes 147464 | tf_op jit(solution)/shard_map/ppermute | solution.py:326
  16.9 0.7 copy-start.12
  17.6 12.0 %copy-start.15 = (s32[16]{0:T(128)S(1)}, s32[16]{0:T(128)}, u32[]{:S(2)}) copy-start(s32[16]{0:T(128)} %param.29) | copy-start | bytes 196
  17.6 33.1 %all-to-all-start = ((bf16[8,272,384]{2,1,0:T(8,128)(2,1)}), bf16[8,272,384]{2,1,0:T(8,128)(2,1)S(1)}, u32[]{:S(2)}, u32[]{:S(2)}) async-start(bf16[8,272,384]{2,1,0:T(8,128)(2,1)} %get-tuple-element.27), calls=%async_computation | async-start | bytes 3342336 | tf_op jit(solution)/shard_map/all_to_all | solution.py:332
  31.6 1.4 copy-start.5
  50.7 1.3 copy-start.4
  50.7 6.3 %copy-start.14 = (f32[16]{0:T(128)S(1)}, f32[16]{0:T(128)}, u32[]{:S(2)}) copy-start(f32[16]{0:T(128)} %param.28) | copy-start | bytes 196
  52.0 27.0 %all-to-all-start.1 = ((bf16[8,272,384]{2,1,0:T(8,128)(2,1)}), bf16[8,272,384]{2,1,0:T(8,128)(2,1)}, u32[]{:S(2)}, u32[]{:S(2)}) async-start(bf16[8,272,384]{2,1,0:T(8,128)(2,1)} %get-tuple-element.35), calls=%async_computation.1 | async-start | bytes 3342336 | tf_op jit(solution)/shard_map/all_to_all | solution.py:351
  70.6 21.5 %collective-permute-start = (bf16[832,128]{1,0:T(8,128)(2,1)}, bf16[832,128]{1,0:T(8,128)(2,1)S(1)}, u32[]{:S(2)}, u32[]{:S(2)}) collective-permute-start(bf16[832,128]{1,0:T(8,128)(2,1)} %get-tuple-element.31), channel_id=1, source_target_pairs={{0,2},{1,3},{2,4},{3,5},{4,6},{5,7},{6,0},{7,1},{8,10},{9,11},{10,... | collective-permute-start | bytes 638984 | tf_op jit(solution)/shard_map/ppermute | solution.py:217
  72.0 21.7 %collective-permute-start.1 = (bf16[832,128]{1,0:T(8,128)(2,1)}, bf16[832,128]{1,0:T(8,128)(2,1)S(1)}, u32[]{:S(2)}, u32[]{:S(2)}) collective-permute-start(bf16[832,128]{1,0:T(8,128)(2,1)} %get-tuple-element.32), channel_id=1, source_target_pairs={{0,4},{1,5},{2,6},{3,7},{4,0},{5,1},{6,2},{7,3},{8,12},{9,13},{10,... | collective-permute-start | bytes 638984 | tf_op jit(solution)/shard_map/ppermute | solution.py:217
  74.4 19.3 %collective-permute-start.2 = (bf16[832,128]{1,0:T(8,128)(2,1)}, bf16[832,128]{1,0:T(8,128)(2,1)S(1)}, u32[]{:S(2)}, u32[]{:S(2)}) collective-permute-start(bf16[832,128]{1,0:T(8,128)(2,1)} %get-tuple-element.33), channel_id=1, source_target_pairs={{0,6},{1,7},{2,0},{3,1},{4,2},{5,3},{6,4},{7,5},{8,14},{9,15},{10,... | collective-permute-start | bytes 638984 | tf_op jit(solution)/shard_map/ppermute | solution.py:217
  90.2 7.7 %collective-permute-start.3 = (bf16[832,128]{1,0:T(8,128)(2,1)}, bf16[832,128]{1,0:T(8,128)(2,1)S(1)}, u32[]{:S(2)}, u32[]{:S(2)}) collective-permute-start(bf16[832,128]{1,0:T(8,128)(2,1)} %get-tuple-element.38), channel_id=1, source_target_pairs={{0,2},{1,3},{2,4},{3,5},{4,6},{5,7},{6,0},{7,1},{8,10},{9,11},{10,... | collective-permute-start | bytes 638984 | tf_op jit(solution)/shard_map/ppermute | solution.py:217
  90.5 10.3 %collective-permute-start.4 = (bf16[832,128]{1,0:T(8,128)(2,1)}, bf16[832,128]{1,0:T(8,128)(2,1)S(1)}, u32[]{:S(2)}, u32[]{:S(2)}) collective-permute-start(bf16[832,128]{1,0:T(8,128)(2,1)} %get-tuple-element.39), channel_id=1, source_target_pairs={{0,4},{1,5},{2,6},{3,7},{4,0},{5,1},{6,2},{7,3},{8,12},{9,13},{10,... | collective-permute-start | bytes 638984 | tf_op jit(solution)/shard_map/ppermute | solution.py:217
  92.2 28.6 %copy-start.6 = (bf16[832,128]{1,0:T(8,128)(2,1)}, bf16[832,128]{1,0:T(8,128)(2,1)S(1)}, u32[]{:S(2)}) copy-start(bf16[832,128]{1,0:T(8,128)(2,1)S(1)} %collective-permute-done.refs_1_) | copy-start | bytes 638980
  92.2 10.7 %collective-permute-start.5 = (bf16[832,128]{1,0:T(8,128)(2,1)}, bf16[832,128]{1,0:T(8,128)(2,1)S(1)}, u32[]{:S(2)}, u32[]{:S(2)}) collective-permute-start(bf16[832,128]{1,0:T(8,128)(2,1)} %get-tuple-element.40), channel_id=1, source_target_pairs={{0,6},{1,7},{2,0},{3,1},{4,2},{5,3},{6,4},{7,5},{8,14},{9,15},{10,... | collective-permute-start | bytes 638984 | tf_op jit(solution)/shard_map/ppermute | solution.py:217
  93.7 27.0 %copy-start.7 = (bf16[832,128]{1,0:T(8,128)(2,1)}, bf16[832,128]{1,0:T(8,128)(2,1)S(1)}, u32[]{:S(2)}) copy-start(bf16[832,128]{1,0:T(8,128)(2,1)S(1)} %collective-permute-done.1.refs_2_) | copy-start | bytes 638980
  93.7 27.0 %copy-start.8 = (bf16[832,128]{1,0:T(8,128)(2,1)}, bf16[832,128]{1,0:T(8,128)(2,1)S(1)}, u32[]{:S(2)}) copy-start(bf16[832,128]{1,0:T(8,128)(2,1)S(1)} %collective-permute-done.2.refs_3_) | copy-start | bytes 638980
  97.8 22.9 %copy-start.9 = (bf16[832,128]{1,0:T(8,128)(2,1)}, bf16[832,128]{1,0:T(8,128)(2,1)S(1)}, u32[]{:S(2)}) copy-start(bf16[832,128]{1,0:T(8,128)(2,1)S(1)} %collective-permute-done.3.refs_5_) | copy-start | bytes 638980
  100.8 20.0 %copy-start.10 = (bf16[832,128]{1,0:T(8,128)(2,1)}, bf16[832,128]{1,0:T(8,128)(2,1)S(1)}, u32[]{:S(2)}) copy-start(bf16[832,128]{1,0:T(8,128)(2,1)S(1)} %collective-permute-done.4.refs_6_) | copy-start | bytes 638980
  102.9 17.8 %copy-start.11 = (bf16[832,128]{1,0:T(8,128)(2,1)}, bf16[832,128]{1,0:T(8,128)(2,1)S(1)}, u32[]{:S(2)}) copy-start(bf16[832,128]{1,0:T(8,128)(2,1)S(1)} %collective-permute-done.5.refs_7_) | copy-start | bytes 638980
  125.2 14.5 %all-to-all-start.2 = ((bf16[8,40,768]{2,1,0:T(8,128)(2,1)}), bf16[8,40,768]{2,1,0:T(8,128)(2,1)S(1)}, u32[]{:S(2)}, u32[]{:S(2)}) async-start(bf16[8,40,768]{2,1,0:T(8,128)(2,1)} %shard_map.170), calls=%async_computation.2 | async-start | bytes 983040 | tf_op jit(solution)/shard_map/all_to_all | solution.py:361
  130.6 13.0 %copy-start.1 = (bf16[1,220,3072]{2,1,0:T(8,128)(2,1)S(1)}, bf16[1,220,3072]{2,1,0:T(8,128)(2,1)}, u32[]{:S(2)}) copy-start(bf16[1,220,3072]{2,1,0:T(8,128)(2,1)} %x.2) | copy-start | bytes 4055044
  139.7 3.8 %collective-permute-start.10 = (bf16[224,3072]{1,0:T(8,128)(2,1)}, bf16[224,3072]{1,0:T(8,128)(2,1)S(1)}, u32[]{:S(2)}, u32[]{:S(2)}) collective-permute-start(bf16[224,3072]{1,0:T(8,128)(2,1)} %get-tuple-element.48), channel_id=1, source_target_pairs={{0,1},{1,0},{2,3},{3,2},{4,5},{5,4},{6,7},{7,6},{8,9},{9,8},{10,11... | collective-permute-start | bytes 4128776 | tf_op jit(solution)/shard_map/ppermute | solution.py:364
  140.6 0.9 copy-start.3
  143.5 1.3 copy-start.2
Sparse Core Ops, SparseCore 0:
  17.7 102.9 all-gather.2

commit v3 on v2

--- a/solution.py
+++ b/solution.py
@@ -137,12 +137,35 @@
     )(chip, scalars, key_rows, qkv, qkv, qkv)
 
 
-def audio_kernel(place, *refs):
-    sources, weight, out, left = refs[: 2 * XS], *refs[2 * XS :]
+def gather_kernel(place, *refs):
+    sources, video, audio = refs[: 2 * XS], refs[2 * XS], refs[2 * XS + 1]
     for number, source in enumerate(sources):
         head, dx = divmod(number, XS)
+        lanes = pl.ds(dx * 256 + head * HEAD_DIM, HEAD_DIM)
+        for half in range(2):
+            side = place[1] if half == 0 else 1 - place[1]
+            low = pl.multiple_of(side * VROWS, 32)
+            video[half * VROWS : (half + 1) * VROWS, lanes] = source[pl.ds(low, VROWS), :]
         low = lax.rem(place[0] - dx + XS, XS) * 256 + head * HEAD_DIM
-        left[:, pl.ds(pl.multiple_of(low, HEAD_DIM), HEAD_DIM)] = source[2 * VROWS :, :]
+        audio[:, pl.ds(pl.multiple_of(low, HEAD_DIM), HEAD_DIM)] = source[2 * VROWS :, :]
+
+
+def gather_rows(place, sources):
+    whole = pl.BlockSpec(memory_space=pltpu.VMEM)
+    return pl.pallas_call(
+        gather_kernel,
+        in_specs=[pl.BlockSpec(memory_space=pltpu.SMEM)] + [whole] * (2 * XS),
+        out_specs=[whole, whole],
+        out_shape=[
+            jax.ShapeDtypeStruct((2 * VROWS, XS * 256), jnp.bfloat16),
+            jax.ShapeDtypeStruct((GROUPS * AROWS, XS * 256), jnp.bfloat16),
+        ],
+        compiler_params=pltpu.CompilerParams(vmem_limit_bytes=VMEM),
+        cost_estimate=pl.CostEstimate(flops=0, bytes_accessed=4_000_000, transcendentals=0),
+    )(place, *sources)
+
+
+def audio_kernel(left, weight, out):
     columns = out.shape[2]
     rows = [weight[x * ZS : (x + 1) * ZS, 0].reshape(columns, 256) for x in range(XS)]
     total = inner(left[...], jnp.concatenate(rows, axis=1))
@@ -150,38 +173,24 @@
         out[device] = total[device * AROWS : device * AROWS + AUD].astype(jnp.bfloat16)
 
 
-def project_audio(place, sources, weights):
+def project_audio(left, weights):
     blocks, slots, width, _ = weights.shape
     out = (GROUPS, AUD, ZS * width)
     return pl.pallas_call(
         audio_kernel,
-        grid_spec=pltpu.PrefetchScalarGridSpec(
-            num_scalar_prefetch=1,
-            grid=(1,),
-            in_specs=[pl.BlockSpec((MESSAGE, HEAD_DIM), lambda n, p: (0, 0))] * (2 * XS)
-            + [pl.BlockSpec((blocks, 1, width, 256), lambda n, p: (0, slots - 1, 0, 0))],
-            out_specs=pl.BlockSpec(out, lambda n, p: (0, 0, 0)),
-            scratch_shapes=[pltpu.VMEM((GROUPS * AROWS, XS * 256), jnp.bfloat16)],
-        ),
+        grid=(1,),
+        in_specs=[
+            pl.BlockSpec(left.shape, lambda n: (0, 0)),
+            pl.BlockSpec((blocks, 1, width, 256), lambda n: (0, slots - 1, 0, 0)),
+        ],
+        out_specs=pl.BlockSpec(out, lambda n: (0, 0, 0)),
         out_shape=jax.ShapeDtypeStruct(out, jnp.bfloat16),
         compiler_params=pltpu.CompilerParams(vmem_limit_bytes=VMEM),
         cost_estimate=pl.CostEstimate(flops=0, bytes_accessed=8_000_000, transcendentals=0),
-    )(place, *sources, weights)
-
-
-def project_kernel(place, *refs):
-    sources, weight, own, other, left = refs[: 2 * XS], *refs[2 * XS :]
-
-    @pl.when(pl.program_id(0) == 0)
-    def _():
-        for half in range(2):
-            side = place[1] if half == 0 else 1 - place[1]
-            low = pl.multiple_of(side * VROWS, 32)
-            for number, source in enumerate(sources):
-                head, dx = divmod(number, XS)
-                lanes = pl.ds(dx * 256 + head * HEAD_DIM, HEAD_DIM)
-                left[half * VROWS : (half + 1) * VROWS, lanes] = source[pl.ds(low, VROWS), :]
-
+    )(left, weights)
+
+
+def project_kernel(left, weight, own, other):
     columns = own.shape[1]
     rows = [weight[:, dx].reshape(columns, 256) for dx in range(XS)]
     total = inner(left[...], jnp.concatenate(rows, axis=1))
@@ -189,27 +198,23 @@
     other[...] = total[VROWS:].astype(jnp.bfloat16)
 
 
-def project(place, sources, weights):
+def project(left, weights):
     width = weights.shape[2]
     step, count = ZS, YS
-    out = pl.BlockSpec((VROWS, step * width), lambda n, p: (0, n))
+    out = pl.BlockSpec((VROWS, step * width), lambda n: (0, n))
     shape = jax.ShapeDtypeStruct((VROWS, count * step * width), jnp.bfloat16)
     return pl.pallas_call(
         project_kernel,
-        grid_spec=pltpu.PrefetchScalarGridSpec(
-            num_scalar_prefetch=1,
-            grid=(count,),
-            in_specs=[pl.BlockSpec((MESSAGE, HEAD_DIM), lambda n, p: (0, 0))] * (2 * XS)
-            + [pl.BlockSpec((step, XS, width, 256), lambda n, p: (n, 0, 0, 0))],
-            out_specs=[out, out],
-            scratch_shapes=[pltpu.VMEM((2 * VROWS, XS * 256), jnp.bfloat16)],
-        ),
+        grid=(count,),
+        in_specs=[
+            pl.BlockSpec(left.shape, lambda n: (0, 0)),
+            pl.BlockSpec((step, XS, width, 256), lambda n: (n, 0, 0, 0)),
+        ],
+        out_specs=[out, out],
         out_shape=[shape, shape],
         compiler_params=pltpu.CompilerParams(vmem_limit_bytes=VMEM),
-        cost_estimate=pl.CostEstimate(
-            flops=0, bytes_accessed=2_000_000 * count, transcendentals=0
-        ),
-    )(place, *sources, weights)
+        cost_estimate=pl.CostEstimate(flops=0, bytes_accessed=8_000_000, transcendentals=0),
+    )(left, weights)
 
 
 def along(array, axis, shift):
@@ -354,12 +359,11 @@
     sent0, done = attention(0, first)
     sent1, _ = attention(1, after(qkv[1], done))
     place = jnp.stack([chip, core])
-    sources = sent0 + sent1
-    parts = project_audio(place, sources, weights)
-    early = list(sources)
-    early[0] = after(sources[0], parts)
+    left_v, left_a = gather_rows(place, sent0 + sent1)
+    parts = project_audio(left_a, weights)
+    left_v = after(left_v, parts)
     parts = lax.all_to_all(parts, "uly", split_axis=0, concat_axis=0, tiled=True)
-    own, other = project(place, early, weights)
+    own, other = project(left_v, weights)
     other, parts = lax.optimization_barrier((other, parts))
     received = lax.ppermute(other, "uly", swap)
     out_audio = finish_audio(parts, x_audio, gate_a)

time: 155 us -> 154 us (level)
  waiting for transfers between devices: 49.2 us -> 46.9 us
    all_gather x1, waiting for transfers between devices: 17.8 us -> 14.2 us  [shards(): lax.all_gather(jnp.stack([block, *near, block_a]), 'dp', axis=0, tiled=Fa...]
    pallas_call x2 -> x3, Pallas kernels: 12.7 us -> 13.5 us  [the longest x1 7.09 us: project(): pl.pallas_call(project_kernel, grid=(count,), in_specs=[pl.BlockSpec(left...]
  transfers between devices with their start and end apart: 15 -> 15, of which waited for: 8 -> 8; matrix products, arithmetic and copies ran while one was open for 3% -> 3% of each run, Pallas kernels for 23% -> 24%
where the time goes in v3:
time: 154 us; the launch traced here: 153 us
  waiting for transfers between devices  46.9 us (30%)
  Pallas kernels  42 us (27%)
  starting transfers between devices  36.7 us (24%)
  between operations  16.1 us (10%)
  local copies, waits for them, and re-layouts  6.59 us (4%)
  other arithmetic  3.93 us (3%)
    pallas_call x2, Pallas kernels, attend(): pl.pallas_call(attend_kernel, grid_spec=pltpu.PrefetchScalarGridSpec(num_...  22.1 us
    all_to_all x1, waiting for transfers between devices, shards(): lax.all_to_all(packed[0], 'uly', split_axis=0, concat_axis=0, tiled=True)  16.8 us
    all_gather x1, waiting for transfers between devices, shards(): lax.all_gather(jnp.stack([block, *near, block_a]), 'dp', axis=0, tiled=Fa...  14.2 us
    ppermute x9, starting transfers between devices, along(): lax.ppermute(array, 'uly', [(i, (i + 2 * shift) % GROUPS) for i in range(...  13.6 us
    all_to_all x1, starting transfers between devices, shards(): lax.all_to_all(packed[0], 'uly', split_axis=0, concat_axis=0, tiled=True)  10.2 us
    ppermute x9, waiting for transfers between devices, along(): lax.ppermute(array, 'uly', [(i, (i + 2 * shift) % GROUPS) for i in range(...  9.21 us
    pallas_call x1, Pallas kernels, project(): pl.pallas_call(project_kernel, grid=(count,), in_specs=[pl.BlockSpec(left...  7.09 us
    unnamed x36, local copies, waits for them, and re-layouts  5.98 us
  transfers between devices with their start and end apart: 15, of which 8 were waited for; matrix products, arithmetic and copies ran while one was open for 3% of the time, Pallas kernels for 24%

profile of v3, /device:TPU:1, one launch (start us, length us, event | category | flops | bytes accessed | tf_op | source)
XLA Modules:
  0.0 152.9 jit_solution(1714103242593982970)
XLA Ops:
  7.2 0.0 copy-start
  7.2 0.0 all-gather.3.cloned.1.call-start
  7.2 2.1 %collective-permute-start.6 = (bf16[96,256]{1,0:T(8,128)(2,1)}, bf16[96,256]{1,0:T(8,128)(2,1)S(1)}, u32[]{:S(2)}, u32[]{:S(2)}) collective-permute-start(bf16[96,256]{1,0:T(8,128)(2,1)} %bitcast.29), channel_id=1, source_target_pairs={{0,2},{1,3},{2,4},{3,5},{4,6},{5,7},{6,0},{7,1},{8,10},{9,11},{10,... | collective-permute-start | bytes 147464 | tf_op jit(solution)/shard_map/ppermute | solution.py:222
  9.3 2.5 %collective-permute-start.7 = (bf16[96,256]{1,0:T(8,128)(2,1)}, bf16[96,256]{1,0:T(8,128)(2,1)S(1)}, u32[]{:S(2)}, u32[]{:S(2)}) collective-permute-start(bf16[96,256]{1,0:T(8,128)(2,1)} %bitcast.30), channel_id=1, source_target_pairs={{0,4},{1,5},{2,6},{3,7},{4,0},{5,1},{6,2},{7,3},{8,12},{9,13},{10,... | collective-permute-start | bytes 147464 | tf_op jit(solution)/shard_map/ppermute | solution.py:222
  11.8 1.2 collective-permute-start.8
  13.0 1.6 %collective-permute-start.9 = (bf16[96,256]{1,0:T(8,128)(2,1)}, bf16[96,256]{1,0:T(8,128)(2,1)S(1)}, u32[]{:S(2)}, u32[]{:S(2)}) collective-permute-start(bf16[96,256]{1,0:T(8,128)(2,1)} %bitcast.33), channel_id=1, source_target_pairs={{0,0},{1,1},{2,64},{3,65},{4,128},{5,129},{6,192},{7,193},{8,8},{9... | collective-permute-start | bytes 147464 | tf_op jit(solution)/shard_map/ppermute | solution.py:331
  14.5 3.4 %shard_map.167 = (bf16[8,272,384]{2,1,0:T(8,128)(2,1)}, bf16[8,272,384]{2,1,0:T(8,128)(2,1)}) custom-call(bf16[1,220,2048]{2,1,0:T(8,128)(2,1)} %refs_0_.1, bf16[1,220,2048]{2,1,0:T(8,128)(2,1)} %refs_1_.1, bf16[1,220,2048]{2,1,0:T(8,128)(2,1)} %refs_2_.1, bf16[1,40,2048]{2,1,0:T(8,128)(2,1)} %refs_3_.1, bf16[1,40,2048]{2,1,0:T(8,128)(2,1)} %refs_4_.1, ...), custom_call_target="tpu_custom_call" | custom-call | bytes 1000000 | tf_op jit(solution)/shard_map/pallas_call | solution.py:55
  18.1 0.7 copy-done.6
  18.8 0.0 all-gather.3.cloned.1.call-update
  18.8 10.2 %all-to-all-start = ((bf16[8,272,384]{2,1,0:T(8,128)(2,1)}), bf16[8,272,384]{2,1,0:T(8,128)(2,1)S(1)}, u32[]{:S(2)}, u32[]{:S(2)}) async-start(bf16[8,272,384]{2,1,0:T(8,128)(2,1)} %get-tuple-element.29), calls=%async_computation | async-start | bytes 3342336 | tf_op jit(solution)/shard_map/all_to_all | solution.py:337
  29.6 0.6 fusion
  31.5 0.1 sine_convert_fusion
  31.6 0.3 fusion.2.gate
  31.9 1.0 copy-done.5
  32.9 0.3 fusion.3.gate
  33.2 0.1 or_select_fusion
  33.3 0.6 pad_maximum_fusion.key_rows
  33.9 16.8 %all-to-all-done.query.keys.values = bf16[8,272,384]{2,1,0:T(8,128)(2,1)S(1)} async-done(((bf16[8,272,384]{2,1,0:T(8,128)(2,1)}), bf16[8,272,384]{2,1,0:T(8,128)(2,1)S(1)}, u32[]{:S(2)}, u32[]{:S(2)}) %all-to-all-start) | async-done | bytes 1671200 | tf_op jit(solution)/shard_map/all_to_all | solution.py:337
  50.7 1.3 copy-done.4
  52.0 5.1 %all-to-all-start.1 = ((bf16[8,272,384]{2,1,0:T(8,128)(2,1)}), bf16[8,272,384]{2,1,0:T(8,128)(2,1)}, u32[]{:S(2)}, u32[]{:S(2)}) async-start(bf16[8,272,384]{2,1,0:T(8,128)(2,1)} %get-tuple-element.37), calls=%async_computation.1 | async-start | bytes 3342336 | tf_op jit(solution)/shard_map/all_to_all | solution.py:356
  57.1 0.6 fusion.1
  57.7 1.9 %pad_maximum_fusion.1 = (f32[2]{0:T(128)}, f32[2]{0:T(128)}) fusion(f32[1]{0:T(128)} %get-tuple-element.57, f32[1]{0:T(128)} %bitcast.3, f32[1]{0:T(128)} %get-tuple-element.56), kind=kLoop, calls=%fused_computation.20 | loop fusion | flops 4 | bytes 28 | tf_op jit(solution)/shard_map/stack | solution.py:350
  59.6 11.0 %shard_map.168 = (bf16[832,128]{1,0:T(8,128)(2,1)}, bf16[832,128]{1,0:T(8,128)(2,1)}, bf16[832,128]{1,0:T(8,128)(2,1)}, bf16[832,128]{1,0:T(8,128)(2,1)}) custom-call(s32[1]{0:T(128)} %bitcast.chip, f32[2]{0:T(128)} %get-tuple-element.58.scalars, f32[2,2176]{1,0:T(2,128)} %pad_maximum_fusion.key_rows, bf16[8,272,384]{2,1,0:T(8,128)(2,1)} %copy-done.4, ...), custom_call_target="tpu_custom_call" | custom-call | bytes 1000000 | tf_op jit(solution)/shard_map/pallas_call | solution.py:120
  70.6 1.4 collective-permute-start
  72.0 2.4 %collective-permute-start.1 = (bf16[832,128]{1,0:T(8,128)(2,1)}, bf16[832,128]{1,0:T(8,128)(2,1)S(1)}, u32[]{:S(2)}, u32[]{:S(2)}) collective-permute-start(bf16[832,128]{1,0:T(8,128)(2,1)} %get-tuple-element.34), channel_id=1, source_target_pairs={{0,4},{1,5},{2,6},{3,7},{4,0},{5,1},{6,2},{7,3},{8,12},{9,13},{10,... | collective-permute-start | bytes 638984 | tf_op jit(solution)/shard_map/ppermute | solution.py:222
  74.4 1.2 collective-permute-start.2
  75.6 3.4 %all-to-all-done.1.query.keys.values = bf16[8,272,384]{2,1,0:T(8,128)(2,1)} async-done(((bf16[8,272,384]{2,1,0:T(8,128)(2,1)}), bf16[8,272,384]{2,1,0:T(8,128)(2,1)}, u32[]{:S(2)}, u32[]{:S(2)}) %all-to-all-start.1) | async-done | bytes 1671200 | tf_op jit(solution)/shard_map/all_to_all | solution.py:356
  79.0 11.1 %shard_map.169 = (bf16[832,128]{1,0:T(8,128)(2,1)}, bf16[832,128]{1,0:T(8,128)(2,1)}, bf16[832,128]{1,0:T(8,128)(2,1)}, bf16[832,128]{1,0:T(8,128)(2,1)}) custom-call(s32[1]{0:T(128)} %bitcast.chip, f32[2]{0:T(128)} %get-tuple-element.59.scalars, f32[2,2176]{1,0:T(2,128)} %pad_maximum_fusion.key_rows, bf16[8,272,384]{2,1,0:T(8,128)(2,1)} %all-to-all-done.1.query.keys.values, ...), custom_call_target="tpu_custom_call" | custom-call | bytes 1000000 | tf_op jit(solution)/shard_map/pallas_call | solution.py:120
  90.1 0.3 collective-permute-start.3
  90.4 1.7 %collective-permute-start.4 = (bf16[832,128]{1,0:T(8,128)(2,1)}, bf16[832,128]{1,0:T(8,128)(2,1)S(1)}, u32[]{:S(2)}, u32[]{:S(2)}) collective-permute-start(bf16[832,128]{1,0:T(8,128)(2,1)} %get-tuple-element.41), channel_id=1, source_target_pairs={{0,4},{1,5},{2,6},{3,7},{4,0},{5,1},{6,2},{7,3},{8,12},{9,13},{10,... | collective-permute-start | bytes 638984 | tf_op jit(solution)/shard_map/ppermute | solution.py:222
  92.1 0.9 collective-permute-start.5
  93.1 0.6 pad_add_fusion.place
  93.7 4.1 %collective-permute-done.3.refs_5_ = bf16[832,128]{1,0:T(8,128)(2,1)S(1)} collective-permute-done((bf16[832,128]{1,0:T(8,128)(2,1)}, bf16[832,128]{1,0:T(8,128)(2,1)S(1)}, u32[]{:S(2)}, u32[]{:S(2)}) %collective-permute-start.3) | collective-permute-done | bytes 213024 | tf_op jit(solution)/shard_map/ppermute | solution.py:222
  97.8 2.9 %collective-permute-done.4.refs_6_ = bf16[832,128]{1,0:T(8,128)(2,1)S(1)} collective-permute-done((bf16[832,128]{1,0:T(8,128)(2,1)}, bf16[832,128]{1,0:T(8,128)(2,1)S(1)}, u32[]{:S(2)}, u32[]{:S(2)}) %collective-permute-start.4) | collective-permute-done | bytes 213024 | tf_op jit(solution)/shard_map/ppermute | solution.py:222
  100.7 2.1 %collective-permute-done.5.refs_7_ = bf16[832,128]{1,0:T(8,128)(2,1)S(1)} collective-permute-done((bf16[832,128]{1,0:T(8,128)(2,1)}, bf16[832,128]{1,0:T(8,128)(2,1)S(1)}, u32[]{:S(2)}, u32[]{:S(2)}) %collective-permute-start.5) | collective-permute-done | bytes 213024 | tf_op jit(solution)/shard_map/ppermute | solution.py:222
  102.9 0.7 copy-done.12
  103.6 3.2 %shard_map.170 = (bf16[448,1024]{1,0:T(8,128)(2,1)}, bf16[384,1024]{1,0:T(8,128)(2,1)}) custom-call(s32[2]{0:T(128)} %pad_add_fusion.place, bf16[832,128]{1,0:T(8,128)(2,1)} %get-tuple-element.32.refs_0_, bf16[832,128]{1,0:T(8,128)(2,1)} %copy-done.7, bf16[832,128]{1,0:T(8,128)(2,1)} %copy-done.8, bf16[832,128]{1,0:T(8,128)(2,1)} %copy-done.9, ...), custom_call_target="tpu_custom_call" | custom-call | bytes 4000000 | tf_op jit(solution)/shard_map/pallas_call | solution.py:155
  106.7 14.2 %all-gather.3.cloned.1.call-done = bf16[160,96,256]{2,1,0:T(8,128)(2,1)} async-done(((bf16[5,96,256]{2,1,0:T(8,128)(2,1)}), bf16[160,96,256]{2,1,0:T(8,128)(2,1)}) %all-gather.3.cloned.1.call-update) | async-done | bytes 7864336 | tf_op jit(solution)/shard_map/all_gather | solution.py:334
  121.0 3.2 %shard_map.171 = bf16[8,40,768]{2,1,0:T(8,128)(2,1)} custom-call(bf16[384,1024]{1,0:T(8,128)(2,1)} %get-tuple-element.44.left, bf16[32,5,96,256]{3,2,1,0:T(8,128)(2,1)} %bitcast.27), custom_call_target="tpu_custom_call" | custom-call | bytes 8000000 | tf_op jit(solution)/shard_map/pallas_call | solution.py:179
  124.2 5.3 %all-to-all-start.2 = ((bf16[8,40,768]{2,1,0:T(8,128)(2,1)}), bf16[8,40,768]{2,1,0:T(8,128)(2,1)S(1)}, u32[]{:S(2)}, u32[]{:S(2)}) async-start(bf16[8,40,768]{2,1,0:T(8,128)(2,1)} %shard_map.171), calls=%async_computation.2 | async-start | bytes 983040 | tf_op jit(solution)/shard_map/all_to_all | solution.py:365
  129.5 7.1 %shard_map.172 = (bf16[224,3072]{1,0:T(8,128)(2,1)}, bf16[224,3072]{1,0:T(8,128)(2,1)}) custom-call(bf16[448,1024]{1,0:T(8,128)(2,1)} %get-tuple-element.49.left, bf16[32,5,96,256]{3,2,1,0:T(8,128)(2,1)} %bitcast.28), custom_call_target="tpu_custom_call" | custom-call | bytes 8000000 | tf_op jit(solution)/shard_map/pallas_call | solution.py:206
  136.6 2.0 %all-to-all-done.2.parts = bf16[8,40,768]{2,1,0:T(8,128)(2,1)S(1)} async-done(((bf16[8,40,768]{2,1,0:T(8,128)(2,1)}), bf16[8,40,768]{2,1,0:T(8,128)(2,1)S(1)}, u32[]{:S(2)}, u32[]{:S(2)}) %all-to-all-start.2) | async-done | bytes 491552 | tf_op jit(solution)/shard_map/all_to_all | solution.py:365
  138.7 0.9 collective-permute-start.10
  139.5 0.9 copy-done.3
  140.5 0.8 shard_map.174
  141.3 1.2 collective-permute-done.10.other
  142.5 1.3 copy-done.2
  143.9 2.2 %shard_map.173 = bf16[1,220,3072]{2,1,0:T(8,128)(2,1)} custom-call(bf16[224,3072]{1,0:T(8,128)(2,1)S(1)} %copy-done.2, bf16[224,3072]{1,0:T(8,128)(2,1)S(1)} %collective-permute-done.10.other, bf16[1,220,3072]{2,1,0:T(8,128)(2,1)S(1)} %copy-done.1, f32[1,3072]{1,0:T(1,128)S(1)} %fusion.2.gate), custom_call_target="tpu_custom_call" | custom-call | bytes 6000000 | tf_op jit(solution)/shard_map/pallas_call | solution.py:248
  (39 shorter events, 0.1 us)
Async XLA Ops:
  7.2 24.4 %copy-start = (bf16[256,3072]{1,0:T(8,128)(2,1)S(1)}, bf16[256,3072]{1,0:T(8,128)(2,1)}, u32[]{:S(2)}) copy-start(bf16[256,3072]{1,0:T(8,128)(2,1)} %param.26) | copy-start | bytes 4718596
  7.2 113.8 %all-gather.3.cloned.1.call-start = ((), (), s32[]{:S(2)}) async-start(), calls=%async_computation.3 | async-start | bytes 8110080 | tf_op jit(solution)/shard_map/all_gather | solution.py:334
  7.2 10.7 %collective-permute-start.6 = (bf16[96,256]{1,0:T(8,128)(2,1)}, bf16[96,256]{1,0:T(8,128)(2,1)S(1)}, u32[]{:S(2)}, u32[]{:S(2)}) collective-permute-start(bf16[96,256]{1,0:T(8,128)(2,1)} %bitcast.29), channel_id=1, source_target_pairs={{0,2},{1,3},{2,4},{3,5},{4,6},{5,7},{6,0},{7,1},{8,10},{9,11},{10,... | collective-permute-start | bytes 147464 | tf_op jit(solution)/shard_map/ppermute | solution.py:222
  9.3 8.6 %collective-permute-start.7 = (bf16[96,256]{1,0:T(8,128)(2,1)}, bf16[96,256]{1,0:T(8,128)(2,1)S(1)}, u32[]{:S(2)}, u32[]{:S(2)}) collective-permute-start(bf16[96,256]{1,0:T(8,128)(2,1)} %bitcast.30), channel_id=1, source_target_pairs={{0,4},{1,5},{2,6},{3,7},{4,0},{5,1},{6,2},{7,3},{8,12},{9,13},{10,... | collective-permute-start | bytes 147464 | tf_op jit(solution)/shard_map/ppermute | solution.py:222
  11.8 6.2 %collective-permute-start.8 = (bf16[96,256]{1,0:T(8,128)(2,1)}, bf16[96,256]{1,0:T(8,128)(2,1)S(1)}, u32[]{:S(2)}, u32[]{:S(2)}) collective-permute-start(bf16[96,256]{1,0:T(8,128)(2,1)} %bitcast.31), channel_id=1, source_target_pairs={{0,6},{1,7},{2,0},{3,1},{4,2},{5,3},{6,4},{7,5},{8,14},{9,15},{10,... | collective-permute-start | bytes 147464 | tf_op jit(solution)/shard_map/ppermute | solution.py:222
  13.0 5.0 %copy-start.13 = (bf16[256,96]{0,1:T(8,128)(2,1)S(1)}, bf16[256,96]{0,1:T(8,128)(2,1)}, u32[]{:S(2)}) copy-start(bf16[256,96]{0,1:T(8,128)(2,1)} %param.24) | copy-start | bytes 147460
  13.0 5.1 %collective-permute-start.9 = (bf16[96,256]{1,0:T(8,128)(2,1)}, bf16[96,256]{1,0:T(8,128)(2,1)S(1)}, u32[]{:S(2)}, u32[]{:S(2)}) collective-permute-start(bf16[96,256]{1,0:T(8,128)(2,1)} %bitcast.33), channel_id=1, source_target_pairs={{0,0},{1,1},{2,64},{3,65},{4,128},{5,129},{6,192},{7,193},{8,8},{9... | collective-permute-start | bytes 147464 | tf_op jit(solution)/shard_map/ppermute | solution.py:331
  18.1 0.7 copy-start.6
  18.8 10.8 %copy-start.15 = (s32[16]{0:T(128)S(1)}, s32[16]{0:T(128)}, u32[]{:S(2)}) copy-start(s32[16]{0:T(128)} %param.29) | copy-start | bytes 196
  18.8 31.9 %all-to-all-start = ((bf16[8,272,384]{2,1,0:T(8,128)(2,1)}), bf16[8,272,384]{2,1,0:T(8,128)(2,1)S(1)}, u32[]{:S(2)}, u32[]{:S(2)}) async-start(bf16[8,272,384]{2,1,0:T(8,128)(2,1)} %get-tuple-element.29), calls=%async_computation | async-start | bytes 3342336 | tf_op jit(solution)/shard_map/all_to_all | solution.py:337
  31.5 1.4 copy-start.5
  50.7 1.3 copy-start.4
  50.7 6.4 %copy-start.14 = (f32[16]{0:T(128)S(1)}, f32[16]{0:T(128)}, u32[]{:S(2)}) copy-start(f32[16]{0:T(128)} %param.28) | copy-start | bytes 196
  52.0 27.0 %all-to-all-start.1 = ((bf16[8,272,384]{2,1,0:T(8,128)(2,1)}), bf16[8,272,384]{2,1,0:T(8,128)(2,1)}, u32[]{:S(2)}, u32[]{:S(2)}) async-start(bf16[8,272,384]{2,1,0:T(8,128)(2,1)} %get-tuple-element.37), calls=%async_computation.1 | async-start | bytes 3342336 | tf_op jit(solution)/shard_map/all_to_all | solution.py:356
  70.6 21.5 %collective-permute-start = (bf16[832,128]{1,0:T(8,128)(2,1)}, bf16[832,128]{1,0:T(8,128)(2,1)S(1)}, u32[]{:S(2)}, u32[]{:S(2)}) collective-permute-start(bf16[832,128]{1,0:T(8,128)(2,1)} %get-tuple-element.33), channel_id=1, source_target_pairs={{0,2},{1,3},{2,4},{3,5},{4,6},{5,7},{6,0},{7,1},{8,10},{9,11},{10,... | collective-permute-start | bytes 638984 | tf_op jit(solution)/shard_map/ppermute | solution.py:222
  72.0 21.7 %collective-permute-start.1 = (bf16[832,128]{1,0:T(8,128)(2,1)}, bf16[832,128]{1,0:T(8,128)(2,1)S(1)}, u32[]{:S(2)}, u32[]{:S(2)}) collective-permute-start(bf16[832,128]{1,0:T(8,128)(2,1)} %get-tuple-element.34), channel_id=1, source_target_pairs={{0,4},{1,5},{2,6},{3,7},{4,0},{5,1},{6,2},{7,3},{8,12},{9,13},{10,... | collective-permute-start | bytes 638984 | tf_op jit(solution)/shard_map/ppermute | solution.py:222
  74.4 19.2 %collective-permute-start.2 = (bf16[832,128]{1,0:T(8,128)(2,1)}, bf16[832,128]{1,0:T(8,128)(2,1)S(1)}, u32[]{:S(2)}, u32[]{:S(2)}) collective-permute-start(bf16[832,128]{1,0:T(8,128)(2,1)} %get-tuple-element.35), channel_id=1, source_target_pairs={{0,6},{1,7},{2,0},{3,1},{4,2},{5,3},{6,4},{7,5},{8,14},{9,15},{10,... | collective-permute-start | bytes 638984 | tf_op jit(solution)/shard_map/ppermute | solution.py:222
  90.1 7.7 %collective-permute-start.3 = (bf16[832,128]{1,0:T(8,128)(2,1)}, bf16[832,128]{1,0:T(8,128)(2,1)S(1)}, u32[]{:S(2)}, u32[]{:S(2)}) collective-permute-start(bf16[832,128]{1,0:T(8,128)(2,1)} %get-tuple-element.40), channel_id=1, source_target_pairs={{0,2},{1,3},{2,4},{3,5},{4,6},{5,7},{6,0},{7,1},{8,10},{9,11},{10,... | collective-permute-start | bytes 638984 | tf_op jit(solution)/shard_map/ppermute | solution.py:222
  90.4 10.3 %collective-permute-start.4 = (bf16[832,128]{1,0:T(8,128)(2,1)}, bf16[832,128]{1,0:T(8,128)(2,1)S(1)}, u32[]{:S(2)}, u32[]{:S(2)}) collective-permute-start(bf16[832,128]{1,0:T(8,128)(2,1)} %get-tuple-element.41), channel_id=1, source_target_pairs={{0,4},{1,5},{2,6},{3,7},{4,0},{5,1},{6,2},{7,3},{8,12},{9,13},{10,... | collective-permute-start | bytes 638984 | tf_op jit(solution)/shard_map/ppermute | solution.py:222
  92.1 10.8 %copy-start.7 = (bf16[832,128]{1,0:T(8,128)(2,1)}, bf16[832,128]{1,0:T(8,128)(2,1)S(1)}, u32[]{:S(2)}) copy-start(bf16[832,128]{1,0:T(8,128)(2,1)S(1)} %collective-permute-done.refs_1_) | copy-start | bytes 638980
  92.1 10.8 %collective-permute-start.5 = (bf16[832,128]{1,0:T(8,128)(2,1)}, bf16[832,128]{1,0:T(8,128)(2,1)S(1)}, u32[]{:S(2)}, u32[]{:S(2)}) collective-permute-start(bf16[832,128]{1,0:T(8,128)(2,1)} %get-tuple-element.42), channel_id=1, source_target_pairs={{0,6},{1,7},{2,0},{3,1},{4,2},{5,3},{6,4},{7,5},{8,14},{9,15},{10,... | collective-permute-start | bytes 638984 | tf_op jit(solution)/shard_map/ppermute | solution.py:222
  93.7 9.2 %copy-start.8 = (bf16[832,128]{1,0:T(8,128)(2,1)}, bf16[832,128]{1,0:T(8,128)(2,1)S(1)}, u32[]{:S(2)}) copy-start(bf16[832,128]{1,0:T(8,128)(2,1)S(1)} %collective-permute-done.1.refs_2_) | copy-start | bytes 638980
  93.7 9.2 %copy-start.9 = (bf16[832,128]{1,0:T(8,128)(2,1)}, bf16[832,128]{1,0:T(8,128)(2,1)S(1)}, u32[]{:S(2)}) copy-start(bf16[832,128]{1,0:T(8,128)(2,1)S(1)} %collective-permute-done.2.refs_3_) | copy-start | bytes 638980
  97.8 5.1 %copy-start.10 = (bf16[832,128]{1,0:T(8,128)(2,1)}, bf16[832,128]{1,0:T(8,128)(2,1)S(1)}, u32[]{:S(2)}) copy-start(bf16[832,128]{1,0:T(8,128)(2,1)S(1)} %collective-permute-done.3.refs_5_) | copy-start | bytes 638980
  100.7 2.2 %copy-start.11 = (bf16[832,128]{1,0:T(8,128)(2,1)}, bf16[832,128]{1,0:T(8,128)(2,1)S(1)}, u32[]{:S(2)}) copy-start(bf16[832,128]{1,0:T(8,128)(2,1)S(1)} %collective-permute-done.4.refs_6_) | copy-start | bytes 638980
  102.9 0.7 copy-start.12
  124.2 14.5 %all-to-all-start.2 = ((bf16[8,40,768]{2,1,0:T(8,128)(2,1)}), bf16[8,40,768]{2,1,0:T(8,128)(2,1)S(1)}, u32[]{:S(2)}, u32[]{:S(2)}) async-start(bf16[8,40,768]{2,1,0:T(8,128)(2,1)} %shard_map.171), calls=%async_computation.2 | async-start | bytes 983040 | tf_op jit(solution)/shard_map/all_to_all | solution.py:365
  129.5 13.0 %copy-start.1 = (bf16[1,220,3072]{2,1,0:T(8,128)(2,1)S(1)}, bf16[1,220,3072]{2,1,0:T(8,128)(2,1)}, u32[]{:S(2)}) copy-start(bf16[1,220,3072]{2,1,0:T(8,128)(2,1)} %x.2) | copy-start | bytes 4055044
  138.7 3.8 %collective-permute-start.10 = (bf16[224,3072]{1,0:T(8,128)(2,1)}, bf16[224,3072]{1,0:T(8,128)(2,1)S(1)}, u32[]{:S(2)}, u32[]{:S(2)}) collective-permute-start(bf16[224,3072]{1,0:T(8,128)(2,1)} %get-tuple-element.52), channel_id=1, source_target_pairs={{0,1},{1,0},{2,3},{3,2},{4,5},{5,4},{6,7},{7,6},{8,9},{9,8},{10,11... | collective-permute-start | bytes 4128776 | tf_op jit(solution)/shard_map/ppermute | solution.py:368
  139.5 0.9 copy-start.3
  142.5 1.3 copy-start.2
Sparse Core Ops, SparseCore 0:
  18.9 101.9 all-gather.2

commit v4 on v3

--- a/solution.py
+++ b/solution.py
@@ -200,7 +200,7 @@
 
 def project(left, weights):
     width = weights.shape[2]
-    step, count = ZS, YS
+    step, count = 2 * ZS, YS // 2
     out = pl.BlockSpec((VROWS, step * width), lambda n: (0, n))
     shape = jax.ShapeDtypeStruct((VROWS, count * step * width), jnp.bfloat16)
     return pl.pallas_call(
@@ -242,12 +242,12 @@
 
 def finish_video(own, other, x, gate):
     total = own.shape[1]
-    step = total // 4
+    step = total // 2
     half = pl.BlockSpec((VROWS, step), lambda n: (0, n))
     video = pl.BlockSpec((1, VID, step), lambda n: (0, 0, n))
     return pl.pallas_call(
         video_kernel,
-        grid=(4,),
+        grid=(2,),
         in_specs=[half, half, video, pl.BlockSpec((1, step), lambda n: (0, n))],
         out_specs=video,
         out_shape=jax.ShapeDtypeStruct(x.shape, jnp.bfloat16),

time: 154 us -> 153 us (level)
  no operation moved by 1% of the time
where the time goes in v4:
time: 153 us; the launch traced here: 152 us
  waiting for transfers between devices  47.5 us (31%)
  Pallas kernels  41 us (27%)
  starting transfers between devices  36.7 us (24%)
  between operations  16.1 us (11%)
  local copies, waits for them, and re-layouts  6.59 us (4%)
  other arithmetic  3.93 us (3%)
    pallas_call x2, Pallas kernels, attend(): pl.pallas_call(attend_kernel, grid_spec=pltpu.PrefetchScalarGridSpec(num_...  22.1 us
    all_to_all x1, waiting for transfers between devices, shards(): lax.all_to_all(packed[0], 'uly', split_axis=0, concat_axis=0, tiled=True)  16.8 us
    all_gather x1, waiting for transfers between devices, shards(): lax.all_gather(jnp.stack([block, *near, block_a]), 'dp', axis=0, tiled=Fa...  14.2 us
    ppermute x9, starting transfers between devices, along(): lax.ppermute(array, 'uly', [(i, (i + 2 * shift) % GROUPS) for i in range(...  13.6 us
    all_to_all x1, starting transfers between devices, shards(): lax.all_to_all(packed[0], 'uly', split_axis=0, concat_axis=0, tiled=True)  10.2 us
    ppermute x9, waiting for transfers between devices, along(): lax.ppermute(array, 'uly', [(i, (i + 2 * shift) % GROUPS) for i in range(...  9.21 us
    pallas_call x1, Pallas kernels, project(): pl.pallas_call(project_kernel, grid=(count,), in_specs=[pl.BlockSpec(left...  6.55 us
    unnamed x36, local copies, waits for them, and re-layouts  5.98 us
  transfers between devices with their start and end apart: 15, of which 8 were waited for; matrix products, arithmetic and copies ran while one was open for 3% of the time, Pallas kernels for 24%

profile of v4, /device:TPU:1, one launch (start us, length us, event | category | flops | bytes accessed | tf_op | source)
XLA Modules:
  0.0 152.5 jit_solution(10935016169658683018)
XLA Ops:
  7.2 0.0 copy-start
  7.2 0.0 all-gather.3.cloned.1.call-start
  7.2 2.1 %collective-permute-start.6 = (bf16[96,256]{1,0:T(8,128)(2,1)}, bf16[96,256]{1,0:T(8,128)(2,1)S(1)}, u32[]{:S(2)}, u32[]{:S(2)}) collective-permute-start(bf16[96,256]{1,0:T(8,128)(2,1)} %bitcast.29), channel_id=1, source_target_pairs={{0,2},{1,3},{2,4},{3,5},{4,6},{5,7},{6,0},{7,1},{8,10},{9,11},{10,... | collective-permute-start | bytes 147464 | tf_op jit(solution)/shard_map/ppermute | solution.py:222
  9.3 2.5 %collective-permute-start.7 = (bf16[96,256]{1,0:T(8,128)(2,1)}, bf16[96,256]{1,0:T(8,128)(2,1)S(1)}, u32[]{:S(2)}, u32[]{:S(2)}) collective-permute-start(bf16[96,256]{1,0:T(8,128)(2,1)} %bitcast.30), channel_id=1, source_target_pairs={{0,4},{1,5},{2,6},{3,7},{4,0},{5,1},{6,2},{7,3},{8,12},{9,13},{10,... | collective-permute-start | bytes 147464 | tf_op jit(solution)/shard_map/ppermute | solution.py:222
  11.8 1.2 collective-permute-start.8
  13.0 1.6 %collective-permute-start.9 = (bf16[96,256]{1,0:T(8,128)(2,1)}, bf16[96,256]{1,0:T(8,128)(2,1)S(1)}, u32[]{:S(2)}, u32[]{:S(2)}) collective-permute-start(bf16[96,256]{1,0:T(8,128)(2,1)} %bitcast.33), channel_id=1, source_target_pairs={{0,0},{1,1},{2,64},{3,65},{4,128},{5,129},{6,192},{7,193},{8,8},{9... | collective-permute-start | bytes 147464 | tf_op jit(solution)/shard_map/ppermute | solution.py:331
  14.5 3.4 %shard_map.167 = (bf16[8,272,384]{2,1,0:T(8,128)(2,1)}, bf16[8,272,384]{2,1,0:T(8,128)(2,1)}) custom-call(bf16[1,220,2048]{2,1,0:T(8,128)(2,1)} %refs_0_.1, bf16[1,220,2048]{2,1,0:T(8,128)(2,1)} %refs_1_.1, bf16[1,220,2048]{2,1,0:T(8,128)(2,1)} %refs_2_.1, bf16[1,40,2048]{2,1,0:T(8,128)(2,1)} %refs_3_.1, bf16[1,40,2048]{2,1,0:T(8,128)(2,1)} %refs_4_.1, ...), custom_call_target="tpu_custom_call" | custom-call | bytes 1000000 | tf_op jit(solution)/shard_map/pallas_call | solution.py:55
  18.1 0.7 copy-done.6
  18.8 0.0 all-gather.3.cloned.1.call-update
  18.8 10.2 %all-to-all-start = ((bf16[8,272,384]{2,1,0:T(8,128)(2,1)}), bf16[8,272,384]{2,1,0:T(8,128)(2,1)S(1)}, u32[]{:S(2)}, u32[]{:S(2)}) async-start(bf16[8,272,384]{2,1,0:T(8,128)(2,1)} %get-tuple-element.29), calls=%async_computation | async-start | bytes 3342336 | tf_op jit(solution)/shard_map/all_to_all | solution.py:337
  29.6 0.6 fusion
  31.5 0.1 sine_convert_fusion
  31.6 0.3 fusion.2.gate
  31.9 1.0 copy-done.5
  32.9 0.3 fusion.3.gate
  33.2 0.1 or_select_fusion
  33.3 0.6 pad_maximum_fusion.key_rows
  33.9 16.8 %all-to-all-done.query.keys.values = bf16[8,272,384]{2,1,0:T(8,128)(2,1)S(1)} async-done(((bf16[8,272,384]{2,1,0:T(8,128)(2,1)}), bf16[8,272,384]{2,1,0:T(8,128)(2,1)S(1)}, u32[]{:S(2)}, u32[]{:S(2)}) %all-to-all-start) | async-done | bytes 1671200 | tf_op jit(solution)/shard_map/all_to_all | solution.py:337
  50.7 1.3 copy-done.4
  52.0 5.1 %all-to-all-start.1 = ((bf16[8,272,384]{2,1,0:T(8,128)(2,1)}), bf16[8,272,384]{2,1,0:T(8,128)(2,1)}, u32[]{:S(2)}, u32[]{:S(2)}) async-start(bf16[8,272,384]{2,1,0:T(8,128)(2,1)} %get-tuple-element.37), calls=%async_computation.1 | async-start | bytes 3342336 | tf_op jit(solution)/shard_map/all_to_all | solution.py:356
  57.1 0.6 fusion.1
  57.7 1.9 %pad_maximum_fusion.1 = (f32[2]{0:T(128)}, f32[2]{0:T(128)}) fusion(f32[1]{0:T(128)} %get-tuple-element.57, f32[1]{0:T(128)} %bitcast.3, f32[1]{0:T(128)} %get-tuple-element.56), kind=kLoop, calls=%fused_computation.20 | loop fusion | flops 4 | bytes 28 | tf_op jit(solution)/shard_map/stack | solution.py:350
  59.6 11.0 %shard_map.168 = (bf16[832,128]{1,0:T(8,128)(2,1)}, bf16[832,128]{1,0:T(8,128)(2,1)}, bf16[832,128]{1,0:T(8,128)(2,1)}, bf16[832,128]{1,0:T(8,128)(2,1)}) custom-call(s32[1]{0:T(128)} %bitcast.chip, f32[2]{0:T(128)} %get-tuple-element.58.scalars, f32[2,2176]{1,0:T(2,128)} %pad_maximum_fusion.key_rows, bf16[8,272,384]{2,1,0:T(8,128)(2,1)} %copy-done.4, ...), custom_call_target="tpu_custom_call" | custom-call | bytes 1000000 | tf_op jit(solution)/shard_map/pallas_call | solution.py:120
  70.6 1.4 collective-permute-start
  72.0 2.4 %collective-permute-start.1 = (bf16[832,128]{1,0:T(8,128)(2,1)}, bf16[832,128]{1,0:T(8,128)(2,1)S(1)}, u32[]{:S(2)}, u32[]{:S(2)}) collective-permute-start(bf16[832,128]{1,0:T(8,128)(2,1)} %get-tuple-element.34), channel_id=1, source_target_pairs={{0,4},{1,5},{2,6},{3,7},{4,0},{5,1},{6,2},{7,3},{8,12},{9,13},{10,... | collective-permute-start | bytes 638984 | tf_op jit(solution)/shard_map/ppermute | solution.py:222
  74.4 1.2 collective-permute-start.2
  75.6 3.4 %all-to-all-done.1.query.keys.values = bf16[8,272,384]{2,1,0:T(8,128)(2,1)} async-done(((bf16[8,272,384]{2,1,0:T(8,128)(2,1)}), bf16[8,272,384]{2,1,0:T(8,128)(2,1)}, u32[]{:S(2)}, u32[]{:S(2)}) %all-to-all-start.1) | async-done | bytes 1671200 | tf_op jit(solution)/shard_map/all_to_all | solution.py:356
  79.0 11.1 %shard_map.169 = (bf16[832,128]{1,0:T(8,128)(2,1)}, bf16[832,128]{1,0:T(8,128)(2,1)}, bf16[832,128]{1,0:T(8,128)(2,1)}, bf16[832,128]{1,0:T(8,128)(2,1)}) custom-call(s32[1]{0:T(128)} %bitcast.chip, f32[2]{0:T(128)} %get-tuple-element.59.scalars, f32[2,2176]{1,0:T(2,128)} %pad_maximum_fusion.key_rows, bf16[8,272,384]{2,1,0:T(8,128)(2,1)} %all-to-all-done.1.query.keys.values, ...), custom_call_target="tpu_custom_call" | custom-call | bytes 1000000 | tf_op jit(solution)/shard_map/pallas_call | solution.py:120
  90.1 0.3 collective-permute-start.3
  90.4 1.7 %collective-permute-start.4 = (bf16[832,128]{1,0:T(8,128)(2,1)}, bf16[832,128]{1,0:T(8,128)(2,1)S(1)}, u32[]{:S(2)}, u32[]{:S(2)}) collective-permute-start(bf16[832,128]{1,0:T(8,128)(2,1)} %get-tuple-element.41), channel_id=1, source_target_pairs={{0,4},{1,5},{2,6},{3,7},{4,0},{5,1},{6,2},{7,3},{8,12},{9,13},{10,... | collective-permute-start | bytes 638984 | tf_op jit(solution)/shard_map/ppermute | solution.py:222
  92.1 0.9 collective-permute-start.5
  93.1 0.6 pad_add_fusion.place
  93.7 4.1 %collective-permute-done.3.refs_5_ = bf16[832,128]{1,0:T(8,128)(2,1)S(1)} collective-permute-done((bf16[832,128]{1,0:T(8,128)(2,1)}, bf16[832,128]{1,0:T(8,128)(2,1)S(1)}, u32[]{:S(2)}, u32[]{:S(2)}) %collective-permute-start.3) | collective-permute-done | bytes 213024 | tf_op jit(solution)/shard_map/ppermute | solution.py:222
  97.8 2.9 %collective-permute-done.4.refs_6_ = bf16[832,128]{1,0:T(8,128)(2,1)S(1)} collective-permute-done((bf16[832,128]{1,0:T(8,128)(2,1)}, bf16[832,128]{1,0:T(8,128)(2,1)S(1)}, u32[]{:S(2)}, u32[]{:S(2)}) %collective-permute-start.4) | collective-permute-done | bytes 213024 | tf_op jit(solution)/shard_map/ppermute | solution.py:222
  100.7 2.1 %collective-permute-done.5.refs_7_ = bf16[832,128]{1,0:T(8,128)(2,1)S(1)} collective-permute-done((bf16[832,128]{1,0:T(8,128)(2,1)}, bf16[832,128]{1,0:T(8,128)(2,1)S(1)}, u32[]{:S(2)}, u32[]{:S(2)}) %collective-permute-start.5) | collective-permute-done | bytes 213024 | tf_op jit(solution)/shard_map/ppermute | solution.py:222
  102.9 0.7 copy-done.12
  103.6 3.2 %shard_map.170 = (bf16[448,1024]{1,0:T(8,128)(2,1)}, bf16[384,1024]{1,0:T(8,128)(2,1)}) custom-call(s32[2]{0:T(128)} %pad_add_fusion.place, bf16[832,128]{1,0:T(8,128)(2,1)} %get-tuple-element.32.refs_0_, bf16[832,128]{1,0:T(8,128)(2,1)} %copy-done.7, bf16[832,128]{1,0:T(8,128)(2,1)} %copy-done.8, bf16[832,128]{1,0:T(8,128)(2,1)} %copy-done.9, ...), custom_call_target="tpu_custom_call" | custom-call | bytes 4000000 | tf_op jit(solution)/shard_map/pallas_call | solution.py:155
  106.7 14.2 %all-gather.3.cloned.1.call-done = bf16[160,96,256]{2,1,0:T(8,128)(2,1)} async-done(((bf16[5,96,256]{2,1,0:T(8,128)(2,1)}), bf16[160,96,256]{2,1,0:T(8,128)(2,1)}) %all-gather.3.cloned.1.call-update) | async-done | bytes 7864336 | tf_op jit(solution)/shard_map/all_gather | solution.py:334
  121.0 3.2 %shard_map.171 = bf16[8,40,768]{2,1,0:T(8,128)(2,1)} custom-call(bf16[384,1024]{1,0:T(8,128)(2,1)} %get-tuple-element.44.left, bf16[32,5,96,256]{3,2,1,0:T(8,128)(2,1)} %bitcast.27), custom_call_target="tpu_custom_call" | custom-call | bytes 8000000 | tf_op jit(solution)/shard_map/pallas_call | solution.py:179
  124.2 5.3 %all-to-all-start.2 = ((bf16[8,40,768]{2,1,0:T(8,128)(2,1)}), bf16[8,40,768]{2,1,0:T(8,128)(2,1)S(1)}, u32[]{:S(2)}, u32[]{:S(2)}) async-start(bf16[8,40,768]{2,1,0:T(8,128)(2,1)} %shard_map.171), calls=%async_computation.2 | async-start | bytes 983040 | tf_op jit(solution)/shard_map/all_to_all | solution.py:365
  129.5 6.6 %shard_map.172 = (bf16[224,3072]{1,0:T(8,128)(2,1)}, bf16[224,3072]{1,0:T(8,128)(2,1)}) custom-call(bf16[448,1024]{1,0:T(8,128)(2,1)} %get-tuple-element.49.left, bf16[32,5,96,256]{3,2,1,0:T(8,128)(2,1)} %bitcast.28), custom_call_target="tpu_custom_call" | custom-call | bytes 8000000 | tf_op jit(solution)/shard_map/pallas_call | solution.py:206
  136.1 2.6 %all-to-all-done.2.parts = bf16[8,40,768]{2,1,0:T(8,128)(2,1)S(1)} async-done(((bf16[8,40,768]{2,1,0:T(8,128)(2,1)}), bf16[8,40,768]{2,1,0:T(8,128)(2,1)S(1)}, u32[]{:S(2)}, u32[]{:S(2)}) %all-to-all-start.2) | async-done | bytes 491552 | tf_op jit(solution)/shard_map/all_to_all | solution.py:365
  138.7 0.9 collective-permute-start.10
  139.5 0.9 copy-done.3
  140.5 0.8 shard_map.174
  141.3 1.2 collective-permute-done.10.other
  142.5 1.3 copy-done.2
  143.9 1.8 %shard_map.173 = bf16[1,220,3072]{2,1,0:T(8,128)(2,1)} custom-call(bf16[224,3072]{1,0:T(8,128)(2,1)S(1)} %copy-done.2, bf16[224,3072]{1,0:T(8,128)(2,1)S(1)} %collective-permute-done.10.other, bf16[1,220,3072]{2,1,0:T(8,128)(2,1)S(1)} %copy-done.1, f32[1,3072]{1,0:T(1,128)S(1)} %fusion.2.gate), custom_call_target="tpu_custom_call" | custom-call | bytes 6000000 | tf_op jit(solution)/shard_map/pallas_call | solution.py:248
  (39 shorter events, 0.1 us)
Async XLA Ops:
  7.2 24.4 %copy-start = (bf16[256,3072]{1,0:T(8,128)(2,1)S(1)}, bf16[256,3072]{1,0:T(8,128)(2,1)}, u32[]{:S(2)}) copy-start(bf16[256,3072]{1,0:T(8,128)(2,1)} %param.26) | copy-start | bytes 4718596
  7.2 113.8 %all-gather.3.cloned.1.call-start = ((), (), s32[]{:S(2)}) async-start(), calls=%async_computation.3 | async-start | bytes 8110080 | tf_op jit(solution)/shard_map/all_gather | solution.py:334
  7.2 10.7 %collective-permute-start.6 = (bf16[96,256]{1,0:T(8,128)(2,1)}, bf16[96,256]{1,0:T(8,128)(2,1)S(1)}, u32[]{:S(2)}, u32[]{:S(2)}) collective-permute-start(bf16[96,256]{1,0:T(8,128)(2,1)} %bitcast.29), channel_id=1, source_target_pairs={{0,2},{1,3},{2,4},{3,5},{4,6},{5,7},{6,0},{7,1},{8,10},{9,11},{10,... | collective-permute-start | bytes 147464 | tf_op jit(solution)/shard_map/ppermute | solution.py:222
  9.3 8.6 %collective-permute-start.7 = (bf16[96,256]{1,0:T(8,128)(2,1)}, bf16[96,256]{1,0:T(8,128)(2,1)S(1)}, u32[]{:S(2)}, u32[]{:S(2)}) collective-permute-start(bf16[96,256]{1,0:T(8,128)(2,1)} %bitcast.30), channel_id=1, source_target_pairs={{0,4},{1,5},{2,6},{3,7},{4,0},{5,1},{6,2},{7,3},{8,12},{9,13},{10,... | collective-permute-start | bytes 147464 | tf_op jit(solution)/shard_map/ppermute | solution.py:222
  11.8 6.2 %collective-permute-start.8 = (bf16[96,256]{1,0:T(8,128)(2,1)}, bf16[96,256]{1,0:T(8,128)(2,1)S(1)}, u32[]{:S(2)}, u32[]{:S(2)}) collective-permute-start(bf16[96,256]{1,0:T(8,128)(2,1)} %bitcast.31), channel_id=1, source_target_pairs={{0,6},{1,7},{2,0},{3,1},{4,2},{5,3},{6,4},{7,5},{8,14},{9,15},{10,... | collective-permute-start | bytes 147464 | tf_op jit(solution)/shard_map/ppermute | solution.py:222
  13.0 5.0 %copy-start.13 = (bf16[256,96]{0,1:T(8,128)(2,1)S(1)}, bf16[256,96]{0,1:T(8,128)(2,1)}, u32[]{:S(2)}) copy-start(bf16[256,96]{0,1:T(8,128)(2,1)} %param.24) | copy-start | bytes 147460
  13.0 5.1 %collective-permute-start.9 = (bf16[96,256]{1,0:T(8,128)(2,1)}, bf16[96,256]{1,0:T(8,128)(2,1)S(1)}, u32[]{:S(2)}, u32[]{:S(2)}) collective-permute-start(bf16[96,256]{1,0:T(8,128)(2,1)} %bitcast.33), channel_id=1, source_target_pairs={{0,0},{1,1},{2,64},{3,65},{4,128},{5,129},{6,192},{7,193},{8,8},{9... | collective-permute-start | bytes 147464 | tf_op jit(solution)/shard_map/ppermute | solution.py:331
  18.1 0.7 copy-start.6
  18.8 10.8 %copy-start.15 = (s32[16]{0:T(128)S(1)}, s32[16]{0:T(128)}, u32[]{:S(2)}) copy-start(s32[16]{0:T(128)} %param.29) | copy-start | bytes 196
  18.8 31.9 %all-to-all-start = ((bf16[8,272,384]{2,1,0:T(8,128)(2,1)}), bf16[8,272,384]{2,1,0:T(8,128)(2,1)S(1)}, u32[]{:S(2)}, u32[]{:S(2)}) async-start(bf16[8,272,384]{2,1,0:T(8,128)(2,1)} %get-tuple-element.29), calls=%async_computation | async-start | bytes 3342336 | tf_op jit(solution)/shard_map/all_to_all | solution.py:337
  31.5 1.4 copy-start.5
  50.7 1.3 copy-start.4
  50.7 6.4 %copy-start.14 = (f32[16]{0:T(128)S(1)}, f32[16]{0:T(128)}, u32[]{:S(2)}) copy-start(f32[16]{0:T(128)} %param.28) | copy-start | bytes 196
  52.0 27.0 %all-to-all-start.1 = ((bf16[8,272,384]{2,1,0:T(8,128)(2,1)}), bf16[8,272,384]{2,1,0:T(8,128)(2,1)}, u32[]{:S(2)}, u32[]{:S(2)}) async-start(bf16[8,272,384]{2,1,0:T(8,128)(2,1)} %get-tuple-element.37), calls=%async_computation.1 | async-start | bytes 3342336 | tf_op jit(solution)/shard_map/all_to_all | solution.py:356
  70.6 21.5 %collective-permute-start = (bf16[832,128]{1,0:T(8,128)(2,1)}, bf16[832,128]{1,0:T(8,128)(2,1)S(1)}, u32[]{:S(2)}, u32[]{:S(2)}) collective-permute-start(bf16[832,128]{1,0:T(8,128)(2,1)} %get-tuple-element.33), channel_id=1, source_target_pairs={{0,2},{1,3},{2,4},{3,5},{4,6},{5,7},{6,0},{7,1},{8,10},{9,11},{10,... | collective-permute-start | bytes 638984 | tf_op jit(solution)/shard_map/ppermute | solution.py:222
  72.0 21.7 %collective-permute-start.1 = (bf16[832,128]{1,0:T(8,128)(2,1)}, bf16[832,128]{1,0:T(8,128)(2,1)S(1)}, u32[]{:S(2)}, u32[]{:S(2)}) collective-permute-start(bf16[832,128]{1,0:T(8,128)(2,1)} %get-tuple-element.34), channel_id=1, source_target_pairs={{0,4},{1,5},{2,6},{3,7},{4,0},{5,1},{6,2},{7,3},{8,12},{9,13},{10,... | collective-permute-start | bytes 638984 | tf_op jit(solution)/shard_map/ppermute | solution.py:222
  74.4 19.2 %collective-permute-start.2 = (bf16[832,128]{1,0:T(8,128)(2,1)}, bf16[832,128]{1,0:T(8,128)(2,1)S(1)}, u32[]{:S(2)}, u32[]{:S(2)}) collective-permute-start(bf16[832,128]{1,0:T(8,128)(2,1)} %get-tuple-element.35), channel_id=1, source_target_pairs={{0,6},{1,7},{2,0},{3,1},{4,2},{5,3},{6,4},{7,5},{8,14},{9,15},{10,... | collective-permute-start | bytes 638984 | tf_op jit(solution)/shard_map/ppermute | solution.py:222
  90.1 7.7 %collective-permute-start.3 = (bf16[832,128]{1,0:T(8,128)(2,1)}, bf16[832,128]{1,0:T(8,128)(2,1)S(1)}, u32[]{:S(2)}, u32[]{:S(2)}) collective-permute-start(bf16[832,128]{1,0:T(8,128)(2,1)} %get-tuple-element.40), channel_id=1, source_target_pairs={{0,2},{1,3},{2,4},{3,5},{4,6},{5,7},{6,0},{7,1},{8,10},{9,11},{10,... | collective-permute-start | bytes 638984 | tf_op jit(solution)/shard_map/ppermute | solution.py:222
  90.4 10.3 %collective-permute-start.4 = (bf16[832,128]{1,0:T(8,128)(2,1)}, bf16[832,128]{1,0:T(8,128)(2,1)S(1)}, u32[]{:S(2)}, u32[]{:S(2)}) collective-permute-start(bf16[832,128]{1,0:T(8,128)(2,1)} %get-tuple-element.41), channel_id=1, source_target_pairs={{0,4},{1,5},{2,6},{3,7},{4,0},{5,1},{6,2},{7,3},{8,12},{9,13},{10,... | collective-permute-start | bytes 638984 | tf_op jit(solution)/shard_map/ppermute | solution.py:222
  92.1 10.8 %copy-start.7 = (bf16[832,128]{1,0:T(8,128)(2,1)}, bf16[832,128]{1,0:T(8,128)(2,1)S(1)}, u32[]{:S(2)}) copy-start(bf16[832,128]{1,0:T(8,128)(2,1)S(1)} %collective-permute-done.refs_1_) | copy-start | bytes 638980
  92.1 10.8 %collective-permute-start.5 = (bf16[832,128]{1,0:T(8,128)(2,1)}, bf16[832,128]{1,0:T(8,128)(2,1)S(1)}, u32[]{:S(2)}, u32[]{:S(2)}) collective-permute-start(bf16[832,128]{1,0:T(8,128)(2,1)} %get-tuple-element.42), channel_id=1, source_target_pairs={{0,6},{1,7},{2,0},{3,1},{4,2},{5,3},{6,4},{7,5},{8,14},{9,15},{10,... | collective-permute-start | bytes 638984 | tf_op jit(solution)/shard_map/ppermute | solution.py:222
  93.7 9.2 %copy-start.8 = (bf16[832,128]{1,0:T(8,128)(2,1)}, bf16[832,128]{1,0:T(8,128)(2,1)S(1)}, u32[]{:S(2)}) copy-start(bf16[832,128]{1,0:T(8,128)(2,1)S(1)} %collective-permute-done.1.refs_2_) | copy-start | bytes 638980
  93.7 9.2 %copy-start.9 = (bf16[832,128]{1,0:T(8,128)(2,1)}, bf16[832,128]{1,0:T(8,128)(2,1)S(1)}, u32[]{:S(2)}) copy-start(bf16[832,128]{1,0:T(8,128)(2,1)S(1)} %collective-permute-done.2.refs_3_) | copy-start | bytes 638980
  97.8 5.1 %copy-start.10 = (bf16[832,128]{1,0:T(8,128)(2,1)}, bf16[832,128]{1,0:T(8,128)(2,1)S(1)}, u32[]{:S(2)}) copy-start(bf16[832,128]{1,0:T(8,128)(2,1)S(1)} %collective-permute-done.3.refs_5_) | copy-start | bytes 638980
  100.7 2.2 %copy-start.11 = (bf16[832,128]{1,0:T(8,128)(2,1)}, bf16[832,128]{1,0:T(8,128)(2,1)S(1)}, u32[]{:S(2)}) copy-start(bf16[832,128]{1,0:T(8,128)(2,1)S(1)} %collective-permute-done.4.refs_6_) | copy-start | bytes 638980
  102.9 0.7 copy-start.12
  124.2 14.5 %all-to-all-start.2 = ((bf16[8,40,768]{2,1,0:T(8,128)(2,1)}), bf16[8,40,768]{2,1,0:T(8,128)(2,1)S(1)}, u32[]{:S(2)}, u32[]{:S(2)}) async-start(bf16[8,40,768]{2,1,0:T(8,128)(2,1)} %shard_map.171), calls=%async_computation.2 | async-start | bytes 983040 | tf_op jit(solution)/shard_map/all_to_all | solution.py:365
  129.5 13.0 %copy-start.1 = (bf16[1,220,3072]{2,1,0:T(8,128)(2,1)S(1)}, bf16[1,220,3072]{2,1,0:T(8,128)(2,1)}, u32[]{:S(2)}) copy-start(bf16[1,220,3072]{2,1,0:T(8,128)(2,1)} %x.2) | copy-start | bytes 4055044
  138.7 3.8 %collective-permute-start.10 = (bf16[224,3072]{1,0:T(8,128)(2,1)}, bf16[224,3072]{1,0:T(8,128)(2,1)S(1)}, u32[]{:S(2)}, u32[]{:S(2)}) collective-permute-start(bf16[224,3072]{1,0:T(8,128)(2,1)} %get-tuple-element.52), channel_id=1, source_target_pairs={{0,1},{1,0},{2,3},{3,2},{4,5},{5,4},{6,7},{7,6},{8,9},{9,8},{10,11... | collective-permute-start | bytes 4128776 | tf_op jit(solution)/shard_map/ppermute | solution.py:368
  139.5 0.9 copy-start.3
  142.5 1.3 copy-start.2
Sparse Core Ops, SparseCore 0:
  18.9 101.9 all-gather.2
